TPU v7x, 512 devices: a whole 4x4x16 slice. The times are simulated.
512 devices in a mesh: blk: 128 (over z, y, core), col: 4 (over x).
Axes of the slice: x: 4, y: 4, z: 16, core: 2. Of those that a mesh axis runs over, the one named last changes fastest.
Arguments:
- panel: float32 [1, 32768, 512], P(None, 'blk')
- trailing: float32 [1, 32768, 2048], P(None, 'blk', 'col'), may hold values from -6 to 6
- pattern: int32 [2, 128], replicated, may hold values from 0 to 1, as said below
- target_rows: int32 [8], P('col'), may hold values from 2 to 127, as said below
Outputs:
- factor: float32 [1, 32768, 512], P(None, 'blk')
- schur_out: float32 [1, 32768, 2048], P(None, 'blk', 'col')
Inputs may be any that keep to these rules, and one draw needn't show every extreme that they name: `pattern`: entries of block rows 0 and 1 are 1; entry (0, 127) is 0. `target_rows`: 8 distinct block rows, among them 2 and 127.
All inputs are finite; a program needn't handle non-finite values.
Results may differ from a plain program's by a relative error of at most 0.00007.
Values sent between devices are 32-bit elements; how exact they have to be, the bound alone decides.
No kernel may reach another device: no remote copies, remote signals or barrier semaphores. Data moves between devices by JAX's collectives and lax.ppermute only.
A program may use at most 64 MiB of HBM per device.

v0:
```python
import jax
import jax.numpy as jnp
from jax import lax
from jax.sharding import PartitionSpec as P


def from_root(block, axis, owner):
    block = jnp.where(lax.axis_index(axis) == owner, block, jnp.zeros_like(block))
    return lax.psum(block, axis)


def right_solve(factor_block, values):
    return lax.linalg.triangular_solve(
        factor_block, values, left_side=False, lower=True, transpose_a=True
    )


def cross_product(left_block, right_block):
    return lax.dot_general(
        left_block, right_block, (((1,), (1,)), ((), ())), precision=lax.Precision.HIGHEST
    )


def solve_rows(raw_rows, first_flag, second_flag, pivot_lead, lower_left, pivot_next, half_width):
    count, height, width = raw_rows.shape
    first_part = (
        raw_rows[:, :, :half_width] * first_flag[:, None, None].astype(jnp.float32)
    ).reshape(count * height, half_width)
    panel_one = right_solve(pivot_lead, first_part)
    second_part = (
        raw_rows[:, :, half_width:] * second_flag[:, None, None].astype(jnp.float32)
    ).reshape(count * height, half_width)
    second_part = second_part - jnp.dot(panel_one, lower_left.T, precision=lax.Precision.HIGHEST)
    panel_two = right_solve(pivot_next, second_part)
    return jnp.concatenate([panel_one, panel_two], axis=1).reshape(count, height, width)


def local(panel, trailing, pattern, target_rows):
    blocks, size_b, panel_width = panel.shape
    half_width = panel_width // 2
    blk_count = lax.axis_size("blk")
    blk_index = lax.axis_index("blk")
    col_count = lax.axis_size("col")
    col_index = lax.axis_index("col")
    total_rows = pattern.shape[1]
    block_ids = jnp.arange(blocks, dtype=jnp.int32) * blk_count + blk_index
    row_table = (jnp.arange(total_rows, dtype=jnp.int32)[None, :] == block_ids[:, None]).astype(
        jnp.int32
    )
    first_flag = jnp.sum(row_table * pattern[0][None, :], axis=1)
    second_flag = jnp.sum(row_table * pattern[1][None, :], axis=1)
    target_count = target_rows.shape[0]
    owners = target_rows % blk_count
    slot_index = target_rows // blk_count
    own_lead = jnp.linalg.cholesky(panel[0, :, :half_width])
    pivot_lead = from_root(own_lead, "blk", 0)
    own_left = right_solve(pivot_lead, panel[0, :, :half_width])
    own_next = jnp.linalg.cholesky(
        panel[0, :, half_width:] - jnp.dot(own_left, own_left.T, precision=lax.Precision.HIGHEST)
    )
    second_row = from_root(jnp.concatenate([own_left, own_next], axis=1), "blk", 1)
    lower_left = second_row[:, :half_width]
    pivot_next = second_row[:, half_width:]
    share_rows = size_b // col_count
    share_start = col_index * share_rows
    my_rows = lax.dynamic_slice_in_dim(panel, share_start, share_rows, 1)
    computed = solve_rows(
        my_rows, first_flag, second_flag, pivot_lead, lower_left, pivot_next, half_width
    )
    top_row = jnp.concatenate([pivot_lead, jnp.zeros_like(pivot_lead)], axis=1)
    next_row = jnp.concatenate([lower_left, pivot_next], axis=1)
    top_share = lax.dynamic_slice_in_dim(top_row, share_start, share_rows, 0)
    next_share = lax.dynamic_slice_in_dim(next_row, share_start, share_rows, 0)
    computed = jnp.where(
        (block_ids == 0)[:, None, None],
        top_share[None],
        jnp.where((block_ids == 1)[:, None, None], next_share[None], computed),
    )
    factor = lax.all_gather(computed, "col", axis=1, tiled=True)
    gathered = []
    for column in range(target_count):
        gathered.append(from_root(factor[slot_index[column]], "blk", owners[column]))
    columns = jnp.stack(gathered)
    keep_rows = block_ids >= 2
    update = cross_product(
        factor.reshape(blocks * size_b, panel_width),
        columns.reshape(target_count * size_b, panel_width),
    )
    update = update.reshape(blocks, size_b, target_count * size_b)
    schur_out = trailing - jnp.where(keep_rows[:, None, None], update, 0.0)
    return (factor, schur_out)


def solution(mesh):
    in_specs = (P(None, "blk", None), P(None, "blk", "col"), P(), P("col"))
    out_specs = (P(None, "blk", None), P(None, "blk", "col"))
    return jax.shard_map(local, mesh=mesh, in_specs=in_specs, out_specs=out_specs, check_vma=False)
```

profile of v0, /device:TPU:1, one launch (start us, length us, event | category | flops | bytes accessed | tf_op | source)
XLA Modules:
  0.0 1154.2 jit_solution(2551082480684097062)
XLA Ops:
  7.2 0.0 all-reduce.7.cloned.1.call-start
  7.2 1.1 fusion.40
  8.3 0.1 copy.17
  8.4 0.9 copy-done
  9.4 11.7 %cholesky.130 = f32[128,128]{1,0:T(8,128)S(1)} custom-call(f32[128,128]{1,0:T(8,128)S(1)} %cholesky.194), custom_call_target="Cholesky" | custom-call | tf_op jit(solution)/shard_map/jit(cholesky)/cholesky | solution.py:55
  21.1 9.8 custom-call.17
  31.0 0.2 constant_dynamic-update-slice_fusion.1
  31.2 0.3 convolution_subtract_fusion.3
  31.5 11.7 %cholesky.147 = f32[128,128]{1,0:T(8,128)S(1)} custom-call(f32[128,128]{1,0:T(8,128)S(1)} %convolution_subtract_fusion.3), custom_call_target="Cholesky" | custom-call | tf_op jit(solution)/shard_map/jit(cholesky)/cholesky | solution.py:55
  43.2 0.6 compare_reduce_fusion.2
  45.2 0.7 select_select_fusion.1
  45.9 0.2 all-reduce.9.cloned.1.call-start
  46.2 0.4 copy-done.4
  46.6 0.7 fusion.34
  47.3 0.6 fusion.41
  48.5 0.1 copy.18
  50.6 328.3 %all-reduce.7.cloned.1.call-done = f32[256,256]{1,0:T(8,128)} async-done(((f32[256,256]{1,0:T(8,128)}), f32[256,256]{1,0:T(8,128)}) %all-reduce.7.cloned.1.call-update) | async-done | bytes 262160 | tf_op jit(solution)/shard_map/psum | solution.py:9
  379.0 1.0 fusion.8
  380.0 0.1 triangular_solve.57
  380.0 4.1 while.5
  380.1 0.6 fusion.56
  380.7 1.4 bitcast_dynamic-update-slice_fusion.4
  382.1 0.6 fusion.56
  382.7 1.4 bitcast_dynamic-update-slice_fusion.4
  384.2 19.7 %custom-call.14 = f32[2,128,128]{1,2,0:T(8,128)S(1)} custom-call(f32[2,128,128]{2,1,0:T(8,128)S(1)} %get-tuple-element.19), custom_call_target="InvertDiagBlocksLowerTriangular" | custom-call | tf_op jit(solution)/shard_map/triangular_solve | solution.py:13
  403.8 0.3 fusion.10
  404.2 0.3 convolution_subtract_fusion.1
  404.4 0.1 copy.8
  404.5 0.4 fusion.28
  404.9 0.4 convolution_subtract_fusion
  405.4 0.1 copy.12
  405.6 11.7 %cholesky.164 = f32[128,128]{1,0:T(8,128)S(1)} custom-call(f32[128,128]{1,0:T(8,128)S(1)} %cholesky.197), custom_call_target="Cholesky" | custom-call | tf_op jit(solution)/shard_map/jit(cholesky)/cholesky | solution.py:58
  417.3 9.8 custom-call.18
  427.1 0.3 fusion.17
  427.4 0.1 copy.13
  427.5 0.3 convolution_subtract_fusion.2
  427.8 0.2 fusion.26
  428.0 11.7 %cholesky.181 = f32[128,128]{1,0:T(8,128)S(1)} custom-call(f32[128,128]{1,0:T(8,128)S(1)} %convolution_subtract_fusion.2), custom_call_target="Cholesky" | custom-call | tf_op jit(solution)/shard_map/jit(cholesky)/cholesky | solution.py:58
  439.8 0.6 compare_reduce_fusion
  440.4 0.6 compare_reduce_fusion.1
  442.4 0.8 maximum_select_fusion
  443.3 0.0 all-reduce.11.cloned.1.call-start
  443.3 0.2 convolution_subtract_fusion.6
  443.6 0.2 fusion.27
  443.8 327.6 %all-reduce.9.cloned.1.call-done = f32[256,512]{1,0:T(8,128)} async-done(((f32[256,512]{1,0:T(8,128)}), f32[256,512]{1,0:T(8,128)}) %all-reduce.9.cloned.1.call-update) | async-done | bytes 524304 | tf_op jit(solution)/shard_map/psum | solution.py:9
  771.3 1.0 slice_select_fusion
  772.4 4.2 while.6
  772.6 0.6 fusion.57
  773.2 1.4 bitcast_dynamic-update-slice_fusion.5
  774.6 0.6 fusion.57
  775.2 1.4 bitcast_dynamic-update-slice_fusion.5
  776.6 19.7 %custom-call.20 = f32[2,128,128]{1,2,0:T(8,128)S(1)} custom-call(f32[2,128,128]{2,1,0:T(8,128)S(1)} %get-tuple-element.27), custom_call_target="InvertDiagBlocksLowerTriangular" | custom-call | tf_op jit(solution)/shard_map/triangular_solve/custom-call.4 | solution.py:13
  796.3 0.4 convolution_subtract_fusion.4
  796.7 0.2 fusion.15
  796.9 0.2 convolution_subtract_fusion.5
  797.1 0.2 fusion.12
  797.3 0.3 copy-done.1
  797.6 10.8 all-gather
  808.5 1.1 select_bitcast_fusion.1
  809.6 334.0 %all-reduce.11.cloned.1.call-done = (f32[1,256,512]{2,1,0:T(8,128)}, f32[1,256,512]{2,1,0:T(8,128)}) async-done(((f32[1,256,512]{2,1,0:T(8,128)}, f32[1,256,512]{2,1,0:T(8,128)}), (f32[1,256,512]{2,1,0:T(8,128)}, f32[1,256,512]{2,1,0:T(8,128)})) %all-reduce.11.cloned.1.call-update) | async-done | bytes 1048592 | tf_op jit(solution)/shard_map/psum | solution.py:9
  1143.6 1.3 pad_maximum_fusion
  1145.0 0.0 copy-done.3
  1145.0 1.9 fusion.1
  1146.9 0.8 copy.46
  (33 shorter events, 0.5 us)
Async XLA Ops:
  7.2 371.8 %all-reduce.7.cloned.1.call-start = ((), (), s32[]{:S(2)}) async-start(), calls=%async_computation | async-start | bytes 524288 | tf_op jit(solution)/shard_map/psum | solution.py:9
  8.3 1.0 copy-start
  45.9 0.7 copy-start.4
  45.9 1.4 copy-start.5
  45.9 725.4 %all-reduce.9.cloned.1.call-start = ((), (), s32[]{:S(2)}) async-start(), calls=%async_computation.1 | async-start | bytes 1048576 | tf_op jit(solution)/shard_map/psum | solution.py:9
  443.3 700.4 %all-reduce.11.cloned.1.call-start = ((), (), s32[]{:S(2)}) async-start(), calls=%async_computation.2 | async-start | bytes 2097152 | tf_op jit(solution)/shard_map/psum | solution.py:9
  771.3 25.0 %copy-start.2 = (f32[256,512]{1,0:T(8,128)S(1)}, f32[256,512]{1,0:T(8,128)}, u32[]{:S(2)}) copy-start(f32[256,512]{1,0:T(8,128)} %all-reduce.9.cloned.1.call-done) | copy-start | bytes 1572868
  796.7 1.0 copy-start.1
  1143.6 1.4 copy-start.3
Sparse Core Ops, SparseCore 0:
  46.0 332.8 all-reduce.6
  443.4 327.8 all-reduce.8
  809.7 333.8 all-reduce.10
where the time goes:
time: 1150 us
  waiting for transfers between devices  990 us (86%)
  other arithmetic  115 us (10%)
  between operations  19.2 us (2%)
  local copies, waits for them, and re-layouts  12.9 us (1%)
    psum x3, waiting for transfers between devices, from_root(): return lax.psum(block, axis)  990 us
    another operation x5, other arithmetic, right_solve(): lax.linalg.triangular_solve(factor_block, values, left_side=False, lower=...  41.4 us
    another operation x7, other arithmetic, local(): jnp.linalg.cholesky(panel[0, :, half_width:] - jnp.dot(own_left, own_left...  34.6 us
    another operation x6, other arithmetic, local(): own_lead = jnp.linalg.cholesky(panel[0, :, :half_width])  34 us
  transfers between devices with their start and end apart: 3, of which 3 were waited for; matrix products, arithmetic and copies ran while one was open for 0% of the time, Pallas kernels for 0%

commit v1 on v0

v1 whole, which is shorter than its diff:
```python
import jax
import jax.numpy as jnp
from jax import lax
from jax.sharding import Mesh, PartitionSpec as P

Z, Y2 = 16, 8


def right_solve(factor_block, values):
    return lax.linalg.triangular_solve(
        factor_block, values, left_side=False, lower=True, transpose_a=True
    )


def hdot(a, b):
    return jnp.dot(a, b, precision=lax.Precision.HIGHEST)


def local(panel, trailing, pattern, target_rows):
    _, size, width = panel.shape
    half = width // 2
    nz, npl, nx = lax.axis_size("z"), lax.axis_size("p"), lax.axis_size("x")
    iz, ip, ix = lax.axis_index("z"), lax.axis_index("p"), lax.axis_index("x")
    row = iz * npl + ip
    count = target_rows.shape[0]
    own = panel[0]
    fine = size // (npl * nx)
    coarse = size // npl
    by_piece = own.reshape(npl, nx, fine, width)
    mine = lax.dynamic_index_in_dim(by_piece, ix, 1, keepdims=False)
    got = lax.all_to_all(mine, "p", 0, 0)
    piece = jnp.concatenate([got[0, :, :half], got[1, :, :half], got[1, :, half:]], axis=0)
    along = lax.all_to_all(jnp.broadcast_to(piece[None], (nz,) + piece.shape), "z", 0, 0)
    piece = along[0]
    full = lax.all_to_all(
        jnp.broadcast_to(piece[None], (npl * nx,) + piece.shape), ("p", "x"), 0, 0
    )
    a00 = full[:, :fine].reshape(size, half)
    a10 = full[:, fine : 2 * fine].reshape(size, half)
    a11 = full[:, 2 * fine :].reshape(size, half)
    pieces = lax.all_to_all(own.reshape(npl, coarse, width), "p", 0, 0)
    sub = coarse // nz
    chosen = jnp.stack(
        [lax.dynamic_index_in_dim(pieces, target_rows[t] % npl, 0, False) for t in range(count)]
    )
    chosen = chosen.reshape(count, nz, sub, width).transpose(1, 0, 2, 3)
    chosen = chosen.reshape(nz, count * sub * width // 128, 128)
    got = lax.all_to_all(chosen, "z", 0, 0)
    got = got.reshape(nz, count, sub * width // 128, 128)
    held = jnp.stack(
        [
            lax.dynamic_index_in_dim(got[:, t], target_rows[t] // npl, 0, False)
            for t in range(count)
        ]
    ).reshape(count * sub * width // 128, 128)
    held = lax.all_to_all(jnp.broadcast_to(held[None], (nz,) + held.shape), "z", 0, 0)
    held = held.reshape(nz, count, sub, width).transpose(1, 0, 2, 3).reshape(count, coarse, width)
    held = lax.all_to_all(jnp.broadcast_to(held[None], (npl,) + held.shape), "p", 0, 0)
    targets = held.transpose(1, 0, 2, 3).reshape(count, size, width)
    l00 = jnp.linalg.cholesky(a00)
    l10 = right_solve(l00, a10)
    l11 = jnp.linalg.cholesky(a11 - hdot(l10, l10.T))
    which = jnp.concatenate([row[None], target_rows])
    hot = (jnp.arange(pattern.shape[1])[None, :] == which[:, None]).astype(jnp.int32)
    flags = jnp.sum(hot[None] * pattern[:, None, :], axis=2).astype(jnp.float32)
    rows = jnp.concatenate([own[None], targets])
    first = (rows[:, :, :half] * flags[0][:, None, None]).reshape(-1, half)
    second = (rows[:, :, half:] * flags[1][:, None, None]).reshape(-1, half)
    one = right_solve(l00, first)
    two = right_solve(l11, second - hdot(one, l10.T))
    solved = jnp.concatenate([one, two], axis=1)
    top = jnp.concatenate([l00, jnp.zeros_like(l00)], axis=1)
    nxt = jnp.concatenate([l10, l11], axis=1)
    mine = jnp.where(row == 0, top, jnp.where(row == 1, nxt, solved[:size]))
    update = lax.dot_general(
        mine, solved[size:], (((1,), (1,)), ((), ())), precision=lax.Precision.HIGHEST
    )
    schur = trailing[0] - jnp.where(row >= 2, update, 0.0)
    return mine[None], schur[None]


def solution(mesh):
    blk, col = mesh.devices.shape
    inner = Mesh(mesh.devices.reshape(blk // Y2, Y2, col), ("z", "p", "x"))
    rows = ("z", "p")
    in_specs = (P(None, rows, None), P(None, rows, "x"), P(), P("x"))
    out_specs = (P(None, rows, None), P(None, rows, "x"))
    return jax.shard_map(local, mesh=inner, in_specs=in_specs, out_specs=out_specs, check_vma=False)
```

time: 1150 us -> 266 us (0.23)
  waiting for transfers between devices: 990 us -> 60.5 us
  starting transfers between devices: 0.3 us -> 57.4 us
    psum x3 -> x0, waiting for transfers between devices: 990 us -> none  [from_root(): return lax.psum(block, axis)]
    all_to_all x0 -> x7, waiting for transfers between devices: none -> 60.5 us  [the longest x1 14.9 us: local(): lax.all_to_all(jnp.broadcast_to(piece[None], (nz,) + piece.shape), 'z', 0...]
    all_to_all x0 -> x7, starting transfers between devices: none -> 57.4 us  [the longest x1 13 us: local(): lax.all_to_all(jnp.broadcast_to(held[None], (nz,) + held.shape), 'z', 0, 0)]
    another operation x15 -> x14, other arithmetic: 71 us -> 68.7 us  [the longest x7 34.6 us: local(): l11 = jnp.linalg.cholesky(a11 - hdot(l10, l10.T))]
  transfers between devices with their start and end apart: 3 -> 7, of which waited for: 3 -> 6; matrix products, arithmetic and copies ran while one was open for 0% -> 47% of each run, Pallas kernels for 0% -> 0%
where the time goes in v1:
time: 266 us; the launch traced here: 265 us
  other arithmetic  110 us (41%)
  waiting for transfers between devices  60.5 us (23%)
  starting transfers between devices  57.4 us (22%)
  local copies, waits for them, and re-layouts  18.1 us (7%)
  matrix products  9.72 us (4%)
  between operations  8.95 us (3%)
    another operation x5, other arithmetic, right_solve(): lax.linalg.triangular_solve(factor_block, values, left_side=False, lower=...  40.3 us
    another operation x7, other arithmetic, local(): l11 = jnp.linalg.cholesky(a11 - hdot(l10, l10.T))  34.6 us
    another operation x6, other arithmetic, local(): l00 = jnp.linalg.cholesky(a00)  34 us
    all_to_all x1, waiting for transfers between devices, local(): lax.all_to_all(jnp.broadcast_to(piece[None], (nz,) + piece.shape), 'z', 0...  14.9 us
    all_to_all x1, starting transfers between devices, local(): lax.all_to_all(jnp.broadcast_to(held[None], (nz,) + held.shape), 'z', 0, 0)  13 us
    all_to_all x1, waiting for transfers between devices, local(): lax.all_to_all(jnp.broadcast_to(piece[None], (npl * nx,) + piece.shape),...  13 us
    all_to_all x1, waiting for transfers between devices, local(): lax.all_to_all(jnp.broadcast_to(held[None], (nz,) + held.shape), 'z', 0, 0)  12 us
    all_to_all x1, waiting for transfers between devices, local(): got = lax.all_to_all(chosen, 'z', 0, 0)  12 us
  transfers between devices with their start and end apart: 7, of which 6 were waited for; matrix products, arithmetic and copies ran while one was open for 47% of the time, Pallas kernels for 0%

profile of v1, /device:TPU:1, one launch (start us, length us, event | category | flops | bytes accessed | tf_op | source)
XLA Modules:
  0.0 265.3 jit_solution(10911012537864605649)
XLA Ops:
  0.6 10.4 %all-to-all-start.3 = ((f32[8,32,512]{2,1,0:T(8,128)}), f32[8,32,512]{2,1,0:T(8,128)S(1)}, u32[]{:S(2)}, u32[]{:S(2)}) async-start(f32[8,32,512]{2,1,0:T(8,128)} %bitcast.128), calls=%async_computation.3 | async-start | bytes 1048576 | tf_op jit(solution)/shard_map/all_to_all | solution.py:41
  11.1 0.6 fusion.44
  15.5 0.7 dynamic-slice_bitcast_fusion
  16.2 4.4 %all-to-all-done.3 = f32[8,32,512]{2,1,0:T(8,128)S(1)} async-done(((f32[8,32,512]{2,1,0:T(8,128)}), f32[8,32,512]{2,1,0:T(8,128)S(1)}, u32[]{:S(2)}, u32[]{:S(2)}) %all-to-all-start.3) | async-done | bytes 524320 | tf_op jit(solution)/shard_map/all_to_all | solution.py:41
  20.6 4.1 %all-to-all-start = ((f32[8,8,512]{2,1,0:T(8,128)}), f32[8,8,512]{2,1,0:T(8,128)S(1)}, u32[]{:S(2)}, u32[]{:S(2)}) async-start(f32[8,8,512]{2,1,0:T(8,128)} %dynamic-slice_bitcast_fusion), calls=%async_computation | async-start | bytes 262144 | tf_op jit(solution)/shard_map/all_to_all | solution.py:31
  24.9 0.8 reshape.86
  25.7 4.3 %all-to-all-done = f32[8,8,512]{2,1,0:T(8,128)S(1)} async-done(((f32[8,8,512]{2,1,0:T(8,128)}), f32[8,8,512]{2,1,0:T(8,128)S(1)}, u32[]{:S(2)}, u32[]{:S(2)}) %all-to-all-start) | async-done | bytes 131104 | tf_op jit(solution)/shard_map/all_to_all | solution.py:31
  30.0 10.6 %all-to-all-start.4 = ((f32[16,16,128]{2,1,0:T(8,128)}), f32[16,16,128]{2,1,0:T(8,128)S(1)}, u32[]{:S(2)}, u32[]{:S(2)}) async-start(f32[16,16,128]{2,1,0:T(8,128)} %reshape.86), calls=%async_computation.4 | async-start | bytes 262144 | tf_op jit(solution)/shard_map/all_to_all | solution.py:48
  40.6 12.0 %all-to-all-done.4 = f32[16,16,128]{2,1,0:T(8,128)S(1)} async-done(((f32[16,16,128]{2,1,0:T(8,128)}), f32[16,16,128]{2,1,0:T(8,128)S(1)}, u32[]{:S(2)}, u32[]{:S(2)}) %all-to-all-start.4) | async-done | bytes 131104 | tf_op jit(solution)/shard_map/all_to_all | solution.py:48
  52.6 0.8 broadcast_in_dim.48
  53.4 5.6 %all-to-all-start.1 = ((f32[16,24,256]{2,1,0:T(8,128)}), f32[16,24,256]{2,1,0:T(8,128)S(1)}, u32[]{:S(2)}, u32[]{:S(2)}) async-start(f32[16,24,256]{2,1,0:T(8,128)} %broadcast_in_dim.48), calls=%async_computation.1 | async-start | bytes 786432 | tf_op jit(solution)/shard_map/all_to_all | solution.py:33
  60.3 14.9 %all-to-all-done.1 = f32[16,24,256]{2,1,0:T(8,128)S(1)} async-done(((f32[16,24,256]{2,1,0:T(8,128)}), f32[16,24,256]{2,1,0:T(8,128)S(1)}, u32[]{:S(2)}, u32[]{:S(2)}) %all-to-all-start.1) | async-done | bytes 393248 | tf_op jit(solution)/shard_map/all_to_all | solution.py:33
  75.2 0.7 broadcast_in_dim.53
  75.9 13.0 %all-to-all-start.5 = ((f32[16,16,128]{2,1,0:T(8,128)}), f32[16,16,128]{2,1,0:T(8,128)S(1)}, u32[]{:S(2)}, u32[]{:S(2)}) async-start(f32[16,16,128]{2,1,0:T(8,128)} %broadcast_in_dim.53), calls=%async_computation.5 | async-start | bytes 262144 | tf_op jit(solution)/shard_map/all_to_all | solution.py:56
  88.9 12.0 %all-to-all-done.5 = f32[16,16,128]{2,1,0:T(8,128)S(1)} async-done(((f32[16,16,128]{2,1,0:T(8,128)}), f32[16,16,128]{2,1,0:T(8,128)S(1)}, u32[]{:S(2)}, u32[]{:S(2)}) %all-to-all-start.5) | async-done | bytes 131104 | tf_op jit(solution)/shard_map/all_to_all | solution.py:56
  100.9 0.9 broadcast_in_dim.50
  101.8 9.2 %all-to-all-start.2 = ((f32[32,24,256]{2,1,0:T(8,128)}), f32[32,24,256]{2,1,0:T(8,128)S(1)}, u32[]{:S(2)}, u32[]{:S(2)}) async-start(f32[32,24,256]{2,1,0:T(8,128)} %broadcast_in_dim.50), calls=%async_computation.2 | async-start | bytes 1572864 | tf_op jit(solution)/shard_map/all_to_all | solution.py:35
  111.7 13.0 %all-to-all-done.2 = f32[32,24,256]{2,1,0:T(8,128)S(1)} async-done(((f32[32,24,256]{2,1,0:T(8,128)}), f32[32,24,256]{2,1,0:T(8,128)S(1)}, u32[]{:S(2)}, u32[]{:S(2)}) %all-to-all-start.2) | async-done | bytes 786464 | tf_op jit(solution)/shard_map/all_to_all | solution.py:35
  124.7 1.1 broadcast_in_dim.55
  125.8 4.4 %all-to-all-start.6 = ((f32[8,2,32,512]{3,2,1,0:T(8,128)}), f32[8,2,32,512]{3,2,1,0:T(8,128)S(1)}, u32[]{:S(2)}, u32[]{:S(2)}) async-start(f32[8,2,32,512]{3,2,1,0:T(8,128)} %broadcast_in_dim.55), calls=%async_computation.6 | async-start | bytes 2097152 | tf_op jit(solution)/shard_map/all_to_all | solution.py:58
  130.2 0.8 slice_bitcast_fusion
  131.2 11.7 %cholesky.130 = f32[128,128]{1,0:T(8,128)S(1)} custom-call(f32[128,128]{1,0:T(8,128)S(1)} %cholesky.194), custom_call_target="Cholesky" | custom-call | tf_op jit(solution)/shard_map/jit(cholesky)/cholesky | solution.py:60
  143.0 9.8 %custom-call.17 = f32[1,128,128]{1,2,0:T(8,128)S(1)} custom-call(f32[1,128,128]{2,1,0:T(8,128)S(1)} %get-tuple-element.73), custom_call_target="InvertDiagBlocksLowerTriangular" | custom-call | tf_op jit(solution)/shard_map/jit(cholesky)/cholesky | solution.py:60
  152.8 0.2 constant_dynamic-update-slice_fusion.1
  153.0 0.3 convolution_subtract_fusion.6
  153.3 11.7 %cholesky.147 = f32[128,128]{1,0:T(8,128)S(1)} custom-call(f32[128,128]{1,0:T(8,128)S(1)} %convolution_subtract_fusion.6), custom_call_target="Cholesky" | custom-call | tf_op jit(solution)/shard_map/jit(cholesky)/cholesky | solution.py:60
  165.0 0.7 compare_reduce_fusion.2
  167.2 4.1 %while.5 = (s32[]{:T(128)}, f32[256,256]{1,0:T(8,128)S(1)}, s32[2,2]{1,0:T(2,128)S(1)}, f32[2,128,128]{2,1,0:T(8,128)S(1)}, s32[]{:T(128)}) while((s32[]{:T(128)}, f32[256,256]{1,0:T(8,128)S(1)}, s32[2,2]{1,0:T(2,128)S(1)}, f32[2,128,128]{2,1,0:T(8,128)S(1)}, s32[]{:T(128)}) %tuple.61), condition=%wide.while_cond.1, body=%wide.while_body.1.sunk | while | flops 2 | bytes 131189 | solution.py:10
  167.2 0.6 fusion.57
  167.8 1.4 bitcast_dynamic-update-slice_fusion.4
  169.3 0.6 fusion.57
  169.9 1.4 bitcast_dynamic-update-slice_fusion.4
  171.3 19.9 %custom-call.14 = f32[2,128,128]{1,2,0:T(8,128)S(1)} custom-call(f32[2,128,128]{2,1,0:T(8,128)S(1)} %get-tuple-element.19), custom_call_target="InvertDiagBlocksLowerTriangular" | custom-call | tf_op jit(solution)/shard_map/triangular_solve | solution.py:10
  191.2 0.3 fusion.21
  191.6 0.4 convolution_subtract_fusion.4
  192.0 0.3 fusion.32
  192.4 0.6 convolution_subtract_fusion.3
  193.2 11.7 %cholesky.164 = f32[128,128]{1,0:T(8,128)S(1)} custom-call(f32[128,128]{1,0:T(8,128)S(1)} %cholesky.197), custom_call_target="Cholesky" | custom-call | tf_op jit(solution)/shard_map/jit(cholesky)/cholesky | solution.py:62
  205.0 9.8 %custom-call.18 = f32[1,128,128]{1,2,0:T(8,128)S(1)} custom-call(f32[1,128,128]{2,1,0:T(8,128)S(1)} %get-tuple-element.69), custom_call_target="InvertDiagBlocksLowerTriangular" | custom-call | tf_op jit(solution)/shard_map/jit(cholesky)/cholesky | solution.py:62
  214.8 0.3 fusion.25
  215.1 0.3 convolution_subtract_fusion.5
  215.6 0.7 copy.102
  216.3 11.7 %cholesky.181 = f32[128,128]{1,0:T(8,128)S(1)} custom-call(f32[128,128]{1,0:T(8,128)S(1)} %convolution_subtract_fusion.5), custom_call_target="Cholesky" | custom-call | tf_op jit(solution)/shard_map/jit(cholesky)/cholesky | solution.py:62
  228.1 0.6 compare_reduce_fusion.1
  228.7 0.7 compare_reduce_fusion
  230.8 4.2 %while.6 = (s32[]{:T(128)}, f32[256,256]{1,0:T(8,128)S(1)}, s32[2,2]{1,0:T(2,128)S(1)}, f32[2,128,128]{2,1,0:T(8,128)S(1)}, s32[]{:T(128)}) while((s32[]{:T(128)}, f32[256,256]{1,0:T(8,128)S(1)}, s32[2,2]{1,0:T(2,128)S(1)}, f32[2,128,128]{2,1,0:T(8,128)S(1)}, s32[]{:T(128)}) %tuple.67), condition=%wide.while_cond.clone, body=%wide.while_body.clone.sunk | while | flops 2 | bytes 131189 | solution.py:10
  231.1 0.6 fusion.58
  231.7 1.4 bitcast_dynamic-update-slice_fusion.5
  233.1 0.6 fusion.58
  233.7 1.4 bitcast_dynamic-update-slice_fusion.5
  235.1 20.3 %custom-call.20 = f32[2,128,128]{1,2,0:T(8,128)} custom-call(f32[2,128,128]{2,1,0:T(8,128)S(1)} %get-tuple-element.27), custom_call_target="InvertDiagBlocksLowerTriangular" | custom-call | tf_op jit(solution)/shard_map/triangular_solve/custom-call.4 | solution.py:10
  255.5 0.2 fusion.7
  255.6 0.7 copy-done.6
  256.4 0.5 fusion.15
  256.9 0.8 convolution_subtract_fusion.2
  257.8 0.5 fusion.31
  258.3 0.8 convolution_subtract_fusion
  259.2 0.5 fusion.13
  259.8 1.6 convolution_subtract_fusion.1
  261.6 0.5 fusion.23
  262.0 0.3 copy-done.2
  262.3 0.9 fusion.40
  263.2 0.3 copy-done.4
  263.5 1.9 fusion.1
  (65 shorter events, 2.5 us)
Async XLA Ops:
  0.6 14.9 %copy-start = (f32[1,256,512]{2,1,0:T(8,128)S(1)}, f32[1,256,512]{2,1,0:T(8,128)}, u32[]{:S(2)}) copy-start(f32[1,256,512]{2,1,0:T(8,128)} %param.7) | copy-start | bytes 1572868
  0.6 10.4 %copy-start.8 = (s32[2]{0:T(128)S(1)}, s32[2]{0:T(128)}, u32[]{:S(2)}) copy-start(s32[2]{0:T(128)} %param.10) | copy-start | bytes 28
  0.6 19.9 %all-to-all-start.3 = ((f32[8,32,512]{2,1,0:T(8,128)}), f32[8,32,512]{2,1,0:T(8,128)S(1)}, u32[]{:S(2)}, u32[]{:S(2)}) async-start(f32[8,32,512]{2,1,0:T(8,128)} %bitcast.128), calls=%async_computation.3 | async-start | bytes 1048576 | tf_op jit(solution)/shard_map/all_to_all | solution.py:41
  20.6 9.4 %all-to-all-start = ((f32[8,8,512]{2,1,0:T(8,128)}), f32[8,8,512]{2,1,0:T(8,128)S(1)}, u32[]{:S(2)}, u32[]{:S(2)}) async-start(f32[8,8,512]{2,1,0:T(8,128)} %dynamic-slice_bitcast_fusion), calls=%async_computation | async-start | bytes 262144 | tf_op jit(solution)/shard_map/all_to_all | solution.py:31
  30.0 22.6 %all-to-all-start.4 = ((f32[16,16,128]{2,1,0:T(8,128)}), f32[16,16,128]{2,1,0:T(8,128)S(1)}, u32[]{:S(2)}, u32[]{:S(2)}) async-start(f32[16,16,128]{2,1,0:T(8,128)} %reshape.86), calls=%async_computation.4 | async-start | bytes 262144 | tf_op jit(solution)/shard_map/all_to_all | solution.py:48
  53.4 21.9 %all-to-all-start.1 = ((f32[16,24,256]{2,1,0:T(8,128)}), f32[16,24,256]{2,1,0:T(8,128)S(1)}, u32[]{:S(2)}, u32[]{:S(2)}) async-start(f32[16,24,256]{2,1,0:T(8,128)} %broadcast_in_dim.48), calls=%async_computation.1 | async-start | bytes 786432 | tf_op jit(solution)/shard_map/all_to_all | solution.py:33
  75.9 25.0 %all-to-all-start.5 = ((f32[16,16,128]{2,1,0:T(8,128)}), f32[16,16,128]{2,1,0:T(8,128)S(1)}, u32[]{:S(2)}, u32[]{:S(2)}) async-start(f32[16,16,128]{2,1,0:T(8,128)} %broadcast_in_dim.53), calls=%async_computation.5 | async-start | bytes 262144 | tf_op jit(solution)/shard_map/all_to_all | solution.py:56
  88.9 22.3 %copy-start.9 = (s32[2,128]{1,0:T(2,128)S(1)}, s32[2,128]{1,0:T(2,128)}, u32[]{:S(2)}) copy-start(s32[2,128]{1,0:T(2,128)} %param.9) | copy-start | bytes 3076
  101.8 22.9 %all-to-all-start.2 = ((f32[32,24,256]{2,1,0:T(8,128)}), f32[32,24,256]{2,1,0:T(8,128)S(1)}, u32[]{:S(2)}, u32[]{:S(2)}) async-start(f32[32,24,256]{2,1,0:T(8,128)} %broadcast_in_dim.50), calls=%async_computation.2 | async-start | bytes 1572864 | tf_op jit(solution)/shard_map/all_to_all | solution.py:35
  125.8 129.5 %all-to-all-start.6 = ((f32[8,2,32,512]{3,2,1,0:T(8,128)}), f32[8,2,32,512]{3,2,1,0:T(8,128)S(1)}, u32[]{:S(2)}, u32[]{:S(2)}) async-start(f32[8,2,32,512]{3,2,1,0:T(8,128)} %broadcast_in_dim.55), calls=%async_computation.6 | async-start | bytes 2097152 | tf_op jit(solution)/shard_map/all_to_all | solution.py:58
  167.1 25.2 %copy-start.3 = (f32[256,256]{1,0:T(8,128)S(1)}, f32[256,256]{1,0:T(8,128)}, u32[]{:S(2)}) copy-start(f32[256,256]{1,0:T(8,128)} %get-tuple-element.56) | copy-start | bytes 786436
  191.2 1.8 copy-start.5
  235.0 20.4 %copy-start.1 = (f32[256,256]{1,0:T(8,128)}, f32[256,256]{1,0:T(8,128)S(1)}, u32[]{:S(2)}) copy-start(f32[256,256]{1,0:T(8,128)S(1)} %get-tuple-element.175) | copy-start | bytes 786436
  255.5 0.9 copy-start.6
  258.3 0.9 copy-start.7
  261.4 0.9 copy-start.2
  262.3 1.2 copy-start.4

commit v2 on v1

v2 whole, which is shorter than its diff:
```python
import jax
import jax.numpy as jnp
from jax import lax
from jax.experimental import pallas as pl
from jax.experimental.pallas import tpu as pltpu
from jax.sharding import Mesh, PartitionSpec as P

PLANE = 8
PANEL = 32
HIGHEST = lax.Precision.HIGHEST
OUTER = (((0,), (0,)), ((), ()))
ROWS = (((1,), (1,)), ((), ()))


def split(x):
    high = x.astype(jnp.bfloat16)
    rest = x - high.astype(jnp.float32)
    mid = rest.astype(jnp.bfloat16)
    low = (rest - mid.astype(jnp.float32)).astype(jnp.bfloat16)
    return high, mid, low


def outer(left, right):
    a, b, c = split(left)
    h, m, l = split(right)
    return lax.dot_general(
        jnp.concatenate([a, a, b, a, b, c], axis=0),
        jnp.concatenate([h, m, h, l, m, h], axis=0),
        OUTER,
        preferred_element_type=jnp.float32,
    )


def recip(d):
    r = pl.reciprocal(d, approx=True)
    return r * (2.0 - d * r)


def lane_block(x, lo, count):
    lane = lax.broadcasted_iota(jnp.int32, x.shape, 1)
    return (lane >= lo) & (lane < lo + count)


def inverse_factor(matrix):
    n = matrix.shape[0]
    groups, tiles = PANEL // 8, n // 128
    sub = lax.broadcasted_iota(jnp.int32, (8, 128), 0)
    lane = lax.broadcasted_iota(jnp.int32, (8, 128), 1)
    rest = matrix
    done = []
    for j in range(n // PANEL):
        lo = PANEL * j
        rows, rest = rest[:PANEL], rest[PANEL:]
        tile, off = lo // 128, lo % 128
        cols = [
            [
                jnp.broadcast_to(rows[8 * g : 8 * g + 8, lo + k : lo + k + 1], (8, 128))
                if g >= k // 8
                else None
                for g in range(groups)
            ]
            for k in range(PANEL)
        ]
        u = [
            [rows[8 * g : 8 * g + 8, 128 * c : 128 * c + 128] for c in range(tiles)]
            for g in range(groups)
        ]
        for g in range(groups):
            eye = (lane - off == sub + 8 * g).astype(jnp.float32)
            u[g][tile] = jnp.where(lane_block(eye, off, PANEL), eye, u[g][tile])
        scale = [jnp.zeros((8, 128), jnp.float32)] * groups
        for k in range(PANEL):
            at, s = k // 8, k % 8
            col = cols[k]
            d = jnp.broadcast_to(col[at][s : s + 1], (8, 128))
            r = recip(d)
            scale[at] = jnp.where(sub == s, lax.rsqrt(d), scale[at])
            if k == PANEL - 1:
                break
            low = [None] * at + [jnp.where(sub > s, col[at], 0.0)] + col[at + 1 :]
            ratio = [None if x is None else x * r for x in low]
            for i in range(k + 1, PANEL):
                first = i // 8
                b = jnp.broadcast_to(col[first][i % 8 : i % 8 + 1], (8, 128))
                for g in range(first, groups):
                    if i == k + 1:
                        cols[i][g] = cols[i][g] - (low[g] * b) * r
                    else:
                        cols[i][g] = cols[i][g] - ratio[g] * b
            for c in range(tiles):
                b = jnp.broadcast_to(u[at][c][s : s + 1], (8, 128))
                for g in range(at if s < 7 else at + 1, groups):
                    u[g][c] = u[g][c] - ratio[g] * b
        u = jnp.concatenate(
            [
                jnp.concatenate([x * scale[g] for x in u[g]], axis=1)
                for g in range(groups)
            ],
            axis=0,
        )
        done.append(u)
        left = rest.shape[0]
        if left:
            update = outer(u[:, 128 * ((lo + PANEL) // 128) :], u)
            update = update[update.shape[0] - left :]
            rest = jnp.where(lane_block(rest, lo, PANEL), 0.0, rest) - update
    full = jnp.concatenate(done, axis=0)
    row = lax.broadcasted_iota(jnp.int32, full.shape, 0)
    column = lax.broadcasted_iota(jnp.int32, full.shape, 1)
    return jnp.where(row >= column, full, 0.0)


def pivot_kernel(a00, a10, a11, lead, below, second):
    inv = inverse_factor(a00[...])
    lead[...] = inv
    l10 = lax.dot_general(
        a10[...], inv, ROWS, precision=HIGHEST, preferred_element_type=jnp.float32
    )
    below[...] = l10
    inner = a11[...] - lax.dot_general(
        l10, l10, ROWS, precision=HIGHEST, preferred_element_type=jnp.float32
    )
    second[...] = inverse_factor(inner)


def pivots(a00, a10, a11):
    like = jax.ShapeDtypeStruct(a00.shape, jnp.float32)
    return pl.pallas_call(
        pivot_kernel,
        out_shape=(like, like, like),
        compiler_params=pltpu.CompilerParams(vmem_limit_bytes=24 << 20),
        cost_estimate=pl.CostEstimate(
            flops=1 << 30, bytes_accessed=6 << 18, transcendentals=0
        ),
    )(a00, a10, a11)


def times_t(a, b):
    return lax.dot_general(a, b, ROWS, precision=lax.Precision.HIGHEST)


def copies(x, count):
    return jnp.broadcast_to(x[None], (count,) + x.shape)


def pick(x, at, axis):
    return lax.dynamic_index_in_dim(x, at, axis, keepdims=False)


def local(panel, trailing, pattern, target_rows):
    _, size, width = panel.shape
    half = width // 2
    nz, npl, nx = lax.axis_size("z"), lax.axis_size("p"), lax.axis_size("x")
    iz, ip, ix = lax.axis_index("z"), lax.axis_index("p"), lax.axis_index("x")
    row = iz * npl + ip
    count = target_rows.shape[0]
    own = panel[0]
    fine, coarse = size // (npl * nx), size // npl
    sub = coarse // nz
    pieces = lax.all_to_all(own.reshape(npl, coarse, width), "p", 0, 0)
    share = lax.dynamic_slice_in_dim(pieces[:2], ix * fine, fine, 1)
    share = jnp.concatenate(
        [share[0, :, :half], share[1, :, :half], share[1, :, half:]], axis=0
    )
    share = jnp.concatenate([share[:, :128], share[:, 128:]], axis=0)
    chosen = jnp.stack([pick(pieces, target_rows[t] % npl, 0) for t in range(count)])
    chosen = chosen.reshape(count, nz, sub, width).transpose(1, 0, 2, 3)
    chosen = chosen.reshape(nz, count * sub * width // 128, 128)
    along = lax.all_to_all(jnp.concatenate([copies(share, nz), chosen], axis=1), "z", 0, 0)
    depth = share.shape[0]
    full = lax.all_to_all(copies(along[0, :depth], npl * nx), ("p", "x"), 0, 0)
    full = full.reshape(npl * nx, 2, 3, fine, 128).transpose(2, 0, 3, 1, 4)
    full = full.reshape(3, size, half)
    lead, l10, second = pivots(full[0], full[1], full[2])
    got = along[:, depth:].reshape(nz, count, sub * width // 128, 128)
    held = jnp.concatenate([pick(got[:, t], target_rows[t] // npl, 0) for t in range(count)])
    held = lax.all_to_all(copies(held, nz), "z", 0, 0)
    held = held.reshape(nz, count, sub, width).transpose(1, 0, 2, 3).reshape(count, coarse, width)
    held = lax.all_to_all(copies(held, npl), "p", 0, 0)
    targets = held.transpose(1, 0, 2, 3).reshape(count * size, width)
    which = jnp.concatenate([row[None], target_rows])
    hot = (jnp.arange(pattern.shape[1])[None, :] == which[:, None]).astype(jnp.int32)
    flags = jnp.sum(hot[None] * pattern[:, None, :], axis=2).astype(jnp.float32)

    def solve(block, flag):
        one = times_t(block[:, :half] * flag[0], lead)
        two = times_t(block[:, half:] * flag[1] - times_t(one, l10), second)
        return one, two

    one, two = solve(own, flags[:, 0])
    lower = jnp.tril(jnp.ones((size, half), jnp.bool_))
    one = jnp.where((row == 0) & ~lower, 0.0, one)
    two = jnp.where((row == 0) | ((row == 1) & ~lower), 0.0, two)
    mine = jnp.concatenate([one, two], axis=1)
    flag = jnp.repeat(flags[:, 1:], size, axis=1)[:, :, None]
    others = jnp.concatenate(solve(targets, flag), axis=1)
    schur = trailing[0] - jnp.where(row >= 2, times_t(mine, others), 0.0)
    return mine[None], schur[None]


def solution(mesh):
    blk, col = mesh.devices.shape
    inner = Mesh(mesh.devices.reshape(blk // PLANE, PLANE, col), ("z", "p", "x"))
    rows = ("z", "p")
    in_specs = (P(None, rows, None), P(None, rows, "x"), P(), P("x"))
    out_specs = (P(None, rows, None), P(None, rows, "x"))
    return jax.shard_map(local, mesh=inner, in_specs=in_specs, out_specs=out_specs, check_vma=False)
```

time: 266 us -> 133 us (0.50)
  other arithmetic: 110 us -> 1.2 us
  Pallas kernels: 0 us -> 14.5 us
  local copies, waits for them, and re-layouts: 18.1 us -> 6.83 us
  starting transfers between devices: 57.4 us -> 46.2 us
  waiting for transfers between devices: 60.5 us -> 50.7 us
  between operations: 8.95 us -> 5.79 us
    another operation x19 -> x1, other arithmetic: 109 us -> 0.01 us  [local(): jnp.stack([pick(pieces, target_rows[t] % npl, 0) for t in range(count)])]
    pallas_call x0 -> x1, Pallas kernels: none -> 14.5 us  [pivots(): pl.pallas_call(pivot_kernel, out_shape=(like, like, like), compiler_param...]
    all_to_all x6 -> x4, starting transfers between devices: 47 us -> 35.9 us  [the longest x1 12.2 us: local(): held = lax.all_to_all(copies(held, nz), 'z', 0, 0)]
    all_to_all x6 -> x4, waiting for transfers between devices: 56.1 us -> 45.3 us  [the longest x1 21.7 us: local(): lax.all_to_all(jnp.concatenate([copies(share, nz), chosen], axis=1), 'z',...]
    another operation x24 -> x1, local copies, waits for them, and re-layouts: 9.44 us -> 0.1 us  [local(): jnp.stack([pick(pieces, target_rows[t] % npl, 0) for t in range(count)])]
    another operation x13 -> x0, matrix products: 6.46 us -> none  [the longest x9 5.41 us: right_solve(): lax.linalg.triangular_solve(factor_block, values, left_side=False, lower=...]
    dot_general x3 -> x7, matrix products: 3.27 us -> 7.17 us  [times_t(): return lax.dot_general(a, b, ROWS, precision=lax.Precision.HIGHEST)]
  transfers between devices with their start and end apart: 7 -> 5, of which waited for: 6 -> 4; matrix products, arithmetic and copies ran while one was open for 47% -> 4% of each run, Pallas kernels for 0% -> 11%
where the time goes in v2:
time: 133 us; the launch traced here: 132 us
  waiting for transfers between devices  50.7 us (38%)
  starting transfers between devices  46.2 us (35%)
  Pallas kernels  14.5 us (11%)
  matrix products  7.17 us (5%)
  local copies, waits for them, and re-layouts  6.83 us (5%)
  between operations  5.79 us (4%)
    all_to_all x1, waiting for transfers between devices, local(): lax.all_to_all(jnp.concatenate([copies(share, nz), chosen], axis=1), 'z',...  21.7 us
    pallas_call x1, Pallas kernels, pivots(): pl.pallas_call(pivot_kernel, out_shape=(like, like, like), compiler_param...  14.5 us
    all_to_all x1, starting transfers between devices, local(): held = lax.all_to_all(copies(held, nz), 'z', 0, 0)  12.2 us
    all_to_all x1, waiting for transfers between devices, local(): held = lax.all_to_all(copies(held, nz), 'z', 0, 0)  11.9 us
    all_to_all x1, waiting for transfers between devices, local(): full = lax.all_to_all(copies(along[0, :depth], npl * nx), ('p', 'x'), 0, 0)  11.8 us
    all_to_all x1, starting transfers between devices, local(): lax.all_to_all(jnp.concatenate([copies(share, nz), chosen], axis=1), 'z',...  10.6 us
    all_to_all x1, starting transfers between devices, local(): pieces = lax.all_to_all(own.reshape(npl, coarse, width), 'p', 0, 0)  10.3 us
    all_to_all x1, starting transfers between devices, local(): full = lax.all_to_all(copies(along[0, :depth], npl * nx), ('p', 'x'), 0, 0)  8.69 us
  transfers between devices with their start and end apart: 5, of which 4 were waited for; matrix products, arithmetic and copies ran while one was open for 4% of the time, Pallas kernels for 11%

profile of v2, /device:TPU:1, one launch (start us, length us, event | category | flops | bytes accessed | tf_op | source)
XLA Modules:
  0.0 132.3 jit_solution(13435480839234705116)
XLA Ops:
  0.6 0.0 copy-start.2
  0.6 10.3 %all-to-all-start = ((f32[8,32,512]{2,1,0:T(8,128)}), f32[8,32,512]{2,1,0:T(8,128)S(1)}, u32[]{:S(2)}, u32[]{:S(2)}) async-start(f32[8,32,512]{2,1,0:T(8,128)} %bitcast.63), calls=%async_computation | async-start | bytes 1048576 | tf_op jit(solution)/shard_map/all_to_all | solution.py:160
  10.9 0.0 copy-done.2
  10.9 0.6 fusion.20
  15.1 5.3 %all-to-all-done = f32[8,32,512]{2,1,0:T(8,128)S(1)} async-done(((f32[8,32,512]{2,1,0:T(8,128)}), f32[8,32,512]{2,1,0:T(8,128)S(1)}, u32[]{:S(2)}, u32[]{:S(2)}) %all-to-all-start) | async-done | bytes 524320 | tf_op jit(solution)/shard_map/all_to_all | solution.py:160
  20.5 0.1 copy.28
  20.6 0.1 copy.29
  20.6 0.1 reshape.71
  20.9 0.8 pad_maximum_fusion
  21.7 10.6 %all-to-all-start.1 = ((f32[16,64,128]{2,1,0:T(8,128)}), f32[16,64,128]{2,1,0:T(8,128)S(1)}, u32[]{:S(2)}, u32[]{:S(2)}) async-start(f32[16,64,128]{2,1,0:T(8,128)} %pad_maximum_fusion), calls=%async_computation.1 | async-start | bytes 1048576 | tf_op jit(solution)/shard_map/all_to_all | solution.py:169
  33.6 21.7 %all-to-all-done.1 = f32[16,64,128]{2,1,0:T(8,128)S(1)} async-done(((f32[16,64,128]{2,1,0:T(8,128)}), f32[16,64,128]{2,1,0:T(8,128)S(1)}, u32[]{:S(2)}, u32[]{:S(2)}) %all-to-all-start.1) | async-done | bytes 524320 | tf_op jit(solution)/shard_map/all_to_all | solution.py:169
  55.3 0.7 broadcast_in_dim.66
  56.0 12.2 %all-to-all-start.3 = ((f32[16,16,128]{2,1,0:T(8,128)}), f32[16,16,128]{2,1,0:T(8,128)S(1)}, u32[]{:S(2)}, u32[]{:S(2)}) async-start(f32[16,16,128]{2,1,0:T(8,128)} %broadcast_in_dim.66), calls=%async_computation.3 | async-start | bytes 262144 | tf_op jit(solution)/shard_map/all_to_all | solution.py:177
  68.1 0.1 pad_add_fusion
  68.2 11.9 %all-to-all-done.3 = f32[16,16,128]{2,1,0:T(8,128)S(1)} async-done(((f32[16,16,128]{2,1,0:T(8,128)}), f32[16,16,128]{2,1,0:T(8,128)S(1)}, u32[]{:S(2)}, u32[]{:S(2)}) %all-to-all-start.3) | async-done | bytes 131104 | tf_op jit(solution)/shard_map/all_to_all | solution.py:177
  80.1 0.9 broadcast_in_dim.64
  81.1 8.7 %all-to-all-start.2 = ((f32[32,48,128]{2,1,0:T(8,128)}), f32[32,48,128]{2,1,0:T(8,128)S(1)}, u32[]{:S(2)}, u32[]{:S(2)}) async-start(f32[32,48,128]{2,1,0:T(8,128)} %broadcast_in_dim.64), calls=%async_computation.2 | async-start | bytes 1572864 | tf_op jit(solution)/shard_map/all_to_all | solution.py:171
  89.8 0.0 copy-start.3
  89.8 0.1 fusion.15
  89.8 0.6 copy-done.3
  90.4 0.1 multiply_reduce_fusion
  90.6 0.2 slice_reduce_fusion
  90.8 0.1 broadcast_bitcast_fusion
  90.9 0.6 fusion.19
  91.5 0.1 reshape.74
  91.5 0.1 copy.30
  91.6 11.8 %all-to-all-done.2 = f32[32,48,128]{2,1,0:T(8,128)S(1)} async-done(((f32[32,48,128]{2,1,0:T(8,128)}), f32[32,48,128]{2,1,0:T(8,128)S(1)}, u32[]{:S(2)}, u32[]{:S(2)}) %all-to-all-start.2) | async-done | bytes 786464 | tf_op jit(solution)/shard_map/all_to_all | solution.py:171
  103.4 1.1 broadcast_in_dim.68
  104.5 4.4 %all-to-all-start.4 = ((f32[8,2,32,512]{3,2,1,0:T(8,128)}), f32[8,2,32,512]{3,2,1,0:T(8,128)S(1)}, u32[]{:S(2)}, u32[]{:S(2)}) async-start(f32[8,2,32,512]{3,2,1,0:T(8,128)} %broadcast_in_dim.68), calls=%async_computation.4 | async-start | bytes 2097152 | tf_op jit(solution)/shard_map/all_to_all | solution.py:179
  109.0 0.1 slice_bitcast_fusion
  109.1 0.0 copy-start
  109.1 14.5 %shard_map.59 = (f32[256,256]{1,0:T(8,128)S(1)}, f32[256,256]{1,0:T(8,128)S(1)}, f32[256,256]{1,0:T(8,128)S(1)}) custom-call(f32[256,256]{1,0:T(8,128)S(1)} %get-tuple-element.24.a00, f32[256,256]{1,0:T(8,128)S(1)} %get-tuple-element.23.a10, f32[256,256]{1,0:T(8,128)S(1)} %get-tuple-element.22.a11), custom_call_target="tpu_custom_call" | custom-call | flops 1073741824 | bytes 1572864 | tf_op jit(solution)/shard_map/pallas_call | solution.py:128
  123.6 0.0 copy-done
  123.6 1.1 fusion.12
  124.6 1.5 %convolution_subtract_fusion.1 = f32[256,256]{1,0:T(8,128)S(1)} fusion(f32[256,256]{0,1:T(8,128)S(1)} %get-tuple-element.39, f32[256,256]{1,0:T(8,128)S(1)} %get-tuple-element.6, f32[256,512]{1,0:T(8,128)S(1)} %bitcast.65, f32[]{:T(128)} %bitcast.18), kind=kOutput, calls=%fused_computation.5 | convolution fusion | flops 201457664 | bytes 1048580 | tf_op jit(solution)/shard_map/dot_general | solution.py:139
  126.1 0.4 convolution_select_fusion.1
  126.6 1.0 copy.33
  127.6 0.0 all-to-all-done.4
  127.6 0.1 copy.32
  127.7 0.7 fusion.5
  128.4 1.0 convolution_subtract_fusion
  129.4 0.0 copy-start.1
  129.4 0.6 fusion.21
  130.1 0.4 copy-done.1
  130.5 1.9 %fusion.1 = f32[1,256,512]{2,1,0:T(8,128)} fusion(f32[512,256]{0,1:T(8,128)S(1)} %fusion.21, f32[512,256]{0,1:T(8,128)S(1)} %fusion.5, f32[1,256,512]{2,1,0:T(8,128)S(1)} %copy-done.1, f32[256,256]{0,1:T(8,128)S(1)} %convolution_select_fusion.1, f32[256,256]{0,1:T(8,128)S(1)} %get-tuple-element.38, pred[]{:T(512)S(6)} %ge.10), kind=kOutput, calls=%fused_computation.2 | convolution fusion | flops 805961728 | bytes 2621441 | tf_op jit(solution)/shard_map/dot_general | solution.py:139
  (18 shorter events, 0.2 us)
Async XLA Ops:
  0.6 10.3 %copy-start.2 = (s32[2]{0:T(128)S(1)}, s32[2]{0:T(128)}, u32[]{:S(2)}) copy-start(s32[2]{0:T(128)} %param.7) | copy-start | bytes 28
  0.6 19.8 %all-to-all-start = ((f32[8,32,512]{2,1,0:T(8,128)}), f32[8,32,512]{2,1,0:T(8,128)S(1)}, u32[]{:S(2)}, u32[]{:S(2)}) async-start(f32[8,32,512]{2,1,0:T(8,128)} %bitcast.63), calls=%async_computation | async-start | bytes 1048576 | tf_op jit(solution)/shard_map/all_to_all | solution.py:160
  21.7 33.5 %all-to-all-start.1 = ((f32[16,64,128]{2,1,0:T(8,128)}), f32[16,64,128]{2,1,0:T(8,128)S(1)}, u32[]{:S(2)}, u32[]{:S(2)}) async-start(f32[16,64,128]{2,1,0:T(8,128)} %pad_maximum_fusion), calls=%async_computation.1 | async-start | bytes 1048576 | tf_op jit(solution)/shard_map/all_to_all | solution.py:169
  56.0 24.2 %all-to-all-start.3 = ((f32[16,16,128]{2,1,0:T(8,128)}), f32[16,16,128]{2,1,0:T(8,128)S(1)}, u32[]{:S(2)}, u32[]{:S(2)}) async-start(f32[16,16,128]{2,1,0:T(8,128)} %broadcast_in_dim.66), calls=%async_computation.3 | async-start | bytes 262144 | tf_op jit(solution)/shard_map/all_to_all | solution.py:177
  81.1 22.4 %all-to-all-start.2 = ((f32[32,48,128]{2,1,0:T(8,128)}), f32[32,48,128]{2,1,0:T(8,128)S(1)}, u32[]{:S(2)}, u32[]{:S(2)}) async-start(f32[32,48,128]{2,1,0:T(8,128)} %broadcast_in_dim.64), calls=%async_computation.2 | async-start | bytes 1572864 | tf_op jit(solution)/shard_map/all_to_all | solution.py:171
  89.8 0.7 copy-start.3
  104.5 23.0 %all-to-all-start.4 = ((f32[8,2,32,512]{3,2,1,0:T(8,128)}), f32[8,2,32,512]{3,2,1,0:T(8,128)S(1)}, u32[]{:S(2)}, u32[]{:S(2)}) async-start(f32[8,2,32,512]{3,2,1,0:T(8,128)} %broadcast_in_dim.68), calls=%async_computation.4 | async-start | bytes 2097152 | tf_op jit(solution)/shard_map/all_to_all | solution.py:179
  109.1 14.5 %copy-start = (f32[1,256,512]{2,1,0:T(8,128)S(1)}, f32[1,256,512]{2,1,0:T(8,128)}, u32[]{:S(2)}) copy-start(f32[1,256,512]{2,1,0:T(8,128)} %param.4) | copy-start | bytes 1572868
  129.4 1.0 copy-start.1

commit v3 on v2

--- a/solution.py
+++ b/solution.py
@@ -7,7 +7,6 @@
 
 PLANE = 8
 PANEL = 32
-HIGHEST = lax.Precision.HIGHEST
 OUTER = (((0,), (0,)), ((), ()))
 ROWS = (((1,), (1,)), ((), ()))
 
@@ -110,33 +109,82 @@
     return jnp.where(row >= column, full, 0.0)
 
 
-def pivot_kernel(a00, a10, a11, lead, below, second):
-    inv = inverse_factor(a00[...])
-    lead[...] = inv
-    l10 = lax.dot_general(
-        a10[...], inv, ROWS, precision=HIGHEST, preferred_element_type=jnp.float32
-    )
+def dot6(left, right):
+    a, b, c = left
+    h, m, l = right
+    return lax.dot_general(
+        jnp.concatenate([a, a, b, a, b, c], axis=1),
+        jnp.concatenate([h, m, h, l, m, h], axis=1),
+        ROWS,
+        preferred_element_type=jnp.float32,
+    )
+
+
+def dot3(left, right):
+    a, b, _ = left
+    h, m, _ = right
+    return lax.dot_general(
+        jnp.concatenate([a, a, b], axis=1),
+        jnp.concatenate([h, m, h], axis=1),
+        ROWS,
+        preferred_element_type=jnp.float32,
+    )
+
+
+def flag(pattern, part, row):
+    return pattern[part, row].astype(jnp.float32)
+
+
+def pivot_kernel(row_ref, pattern, blocks, own, lead, below, second, mine):
+    size, width = own.shape
+    half = width // 2
+    row = row_ref[0]
+    w00 = inverse_factor(blocks[:, 0].reshape(size, half))
+    lead[...] = w00
+    w00 = split(w00)
+    l10 = dot6(split(blocks[:, 1].reshape(size, half)), w00)
     below[...] = l10
-    inner = a11[...] - lax.dot_general(
-        l10, l10, ROWS, precision=HIGHEST, preferred_element_type=jnp.float32
-    )
-    second[...] = inverse_factor(inner)
-
-
-def pivots(a00, a10, a11):
-    like = jax.ShapeDtypeStruct(a00.shape, jnp.float32)
+    l10 = split(l10)
+    w11 = inverse_factor(blocks[:, 2].reshape(size, half) - dot6(l10, l10))
+    second[...] = w11
+    w11 = split(w11)
+    one = dot6(split(own[:, :half] * flag(pattern, 0, row)), w00)
+    inner = own[:, half:] * flag(pattern, 1, row) - dot6(split(one), l10)
+    two = dot6(split(inner), w11)
+    shape = (size, half)
+    upper = lax.broadcasted_iota(jnp.int32, shape, 0) < lax.broadcasted_iota(jnp.int32, shape, 1)
+    mine[:, :half] = jnp.where(upper & (row == 0), 0.0, one)
+    mine[:, half:] = jnp.where((upper & (row == 1)) | (row == 0), 0.0, two)
+
+
+def update_kernel(row_ref, pattern, rows, targets, lead, below, second, mine, trailing, out):
+    size, width = mine.shape
+    half = width // 2
+    w00, l10, w11 = split(lead[...]), split(below[...]), split(second[...])
+    left, right = split(mine[:, :half]), split(mine[:, half:])
+    keep = (row_ref[0] >= 2).astype(jnp.float32)
+    for t in range(targets.shape[1]):
+        block = targets[:, t].reshape(size, width)
+        one = split(dot3(split(block[:, :half] * flag(pattern, 0, rows[t])), w00))
+        inner = block[:, half:] * flag(pattern, 1, rows[t]) - dot3(one, l10)
+        two = split(dot3(split(inner), w11))
+        update = dot3(left, one) + dot3(right, two)
+        at = slice(t * size, (t + 1) * size)
+        out[:, at] = trailing[:, at] - keep * update
+
+
+def call(kernel, scalars, arrays, shapes, flops):
+    specs = [pl.BlockSpec(memory_space=pltpu.SMEM)] * len(scalars)
+    specs += [pl.BlockSpec(memory_space=pltpu.VMEM)] * len(arrays)
+    outs = [jax.ShapeDtypeStruct(shape, jnp.float32) for shape in shapes]
     return pl.pallas_call(
-        pivot_kernel,
-        out_shape=(like, like, like),
-        compiler_params=pltpu.CompilerParams(vmem_limit_bytes=24 << 20),
-        cost_estimate=pl.CostEstimate(
-            flops=1 << 30, bytes_accessed=6 << 18, transcendentals=0
-        ),
-    )(a00, a10, a11)
-
-
-def times_t(a, b):
-    return lax.dot_general(a, b, ROWS, precision=lax.Precision.HIGHEST)
+        kernel,
+        in_specs=specs,
+        out_specs=[pl.BlockSpec(memory_space=pltpu.VMEM)] * len(outs),
+        out_shape=outs,
+        compiler_params=pltpu.CompilerParams(vmem_limit_bytes=32 << 20),
+        cost_estimate=pl.CostEstimate(flops=flops, bytes_accessed=1 << 20, transcendentals=0),
+    )(*scalars, *arrays)
 
 
 def copies(x, count):
@@ -150,51 +198,42 @@
 def local(panel, trailing, pattern, target_rows):
     _, size, width = panel.shape
     half = width // 2
-    nz, npl, nx = lax.axis_size("z"), lax.axis_size("p"), lax.axis_size("x")
-    iz, ip, ix = lax.axis_index("z"), lax.axis_index("p"), lax.axis_index("x")
-    row = iz * npl + ip
+    nz, npl = lax.axis_size("z"), lax.axis_size("p")
+    row = (lax.axis_index("z") * npl + lax.axis_index("p")).astype(jnp.int32)[None]
     count = target_rows.shape[0]
     own = panel[0]
-    fine, coarse = size // (npl * nx), size // npl
-    sub = coarse // nz
+    coarse, lanes = size // npl, width // 128
+    sub = coarse * lanes // nz
     pieces = lax.all_to_all(own.reshape(npl, coarse, width), "p", 0, 0)
-    share = lax.dynamic_slice_in_dim(pieces[:2], ix * fine, fine, 1)
-    share = jnp.concatenate(
-        [share[0, :, :half], share[1, :, :half], share[1, :, half:]], axis=0
-    )
-    share = jnp.concatenate([share[:, :128], share[:, 128:]], axis=0)
-    chosen = jnp.stack([pick(pieces, target_rows[t] % npl, 0) for t in range(count)])
-    chosen = chosen.reshape(count, nz, sub, width).transpose(1, 0, 2, 3)
-    chosen = chosen.reshape(nz, count * sub * width // 128, 128)
-    along = lax.all_to_all(jnp.concatenate([copies(share, nz), chosen], axis=1), "z", 0, 0)
-    depth = share.shape[0]
-    full = lax.all_to_all(copies(along[0, :depth], npl * nx), ("p", "x"), 0, 0)
-    full = full.reshape(npl * nx, 2, 3, fine, 128).transpose(2, 0, 3, 1, 4)
-    full = full.reshape(3, size, half)
-    lead, l10, second = pivots(full[0], full[1], full[2])
-    got = along[:, depth:].reshape(nz, count, sub * width // 128, 128)
-    held = jnp.concatenate([pick(got[:, t], target_rows[t] // npl, 0) for t in range(count)])
-    held = lax.all_to_all(copies(held, nz), "z", 0, 0)
-    held = held.reshape(nz, count, sub, width).transpose(1, 0, 2, 3).reshape(count, coarse, width)
-    held = lax.all_to_all(copies(held, npl), "p", 0, 0)
-    targets = held.transpose(1, 0, 2, 3).reshape(count * size, width)
-    which = jnp.concatenate([row[None], target_rows])
-    hot = (jnp.arange(pattern.shape[1])[None, :] == which[:, None]).astype(jnp.int32)
-    flags = jnp.sum(hot[None] * pattern[:, None, :], axis=2).astype(jnp.float32)
-
-    def solve(block, flag):
-        one = times_t(block[:, :half] * flag[0], lead)
-        two = times_t(block[:, half:] * flag[1] - times_t(one, l10), second)
-        return one, two
-
-    one, two = solve(own, flags[:, 0])
-    lower = jnp.tril(jnp.ones((size, half), jnp.bool_))
-    one = jnp.where((row == 0) & ~lower, 0.0, one)
-    two = jnp.where((row == 0) | ((row == 1) & ~lower), 0.0, two)
-    mine = jnp.concatenate([one, two], axis=1)
-    flag = jnp.repeat(flags[:, 1:], size, axis=1)[:, :, None]
-    others = jnp.concatenate(solve(targets, flag), axis=1)
-    schur = trailing[0] - jnp.where(row >= 2, times_t(mine, others), 0.0)
+    chosen = [pieces[0], pieces[1]]
+    chosen += [pick(pieces, target_rows[t] % npl, 0) for t in range(count)]
+    wanted = len(chosen)
+    chosen = jnp.stack(chosen).reshape(wanted, coarse // sub, sub, lanes, 128)
+    chosen = chosen.transpose(1, 3, 0, 2, 4).reshape(nz, wanted * sub, 128)
+    got = lax.all_to_all(chosen, "z", 0, 0).reshape(nz, wanted, sub, 128)
+    held = [got[0, 0], got[0, 1]]
+    held += [pick(got[:, 2 + t], target_rows[t] // npl, 0) for t in range(count)]
+    held = lax.all_to_all(copies(jnp.concatenate(held), nz), "z", 0, 0)
+    held = held.reshape(coarse // sub, lanes, wanted, sub, 128).transpose(2, 0, 3, 1, 4)
+    held = held.reshape(wanted, coarse, width)
+    blocks = jnp.stack([held[0, :, :half], held[1, :, :half], held[1, :, half:]])
+    blocks = lax.all_to_all(copies(blocks, npl), "p", 0, 0)
+    targets = lax.all_to_all(copies(held[2:], npl), "p", 0, 0)
+    square = (size, half)
+    lead, below, second, mine = call(
+        pivot_kernel,
+        (row, pattern),
+        (blocks, own),
+        (square, square, square, (size, width)),
+        1 << 34,
+    )
+    (schur,) = call(
+        update_kernel,
+        (row, pattern, target_rows),
+        (targets, lead, below, second, mine, trailing[0]),
+        ((size, trailing.shape[2]),),
+        1 << 30,
+    )
     return mine[None], schur[None]
 
 

time: 133 us -> 121 us (0.910)
  blocking collectives: 0 us -> 24 us
  waiting for transfers between devices: 50.7 us -> 29.3 us
  starting transfers between devices: 46.2 us -> 35.1 us
  matrix products: 7.17 us -> 0 us
  Pallas kernels: 14.5 us -> 19.6 us
    all_to_all x0 -> x1, blocking collectives: none -> 24 us  [local(): held = lax.all_to_all(copies(jnp.concatenate(held), nz), 'z', 0, 0)]
    all_to_all x4 -> x3, waiting for transfers between devices: 45.3 us -> 24 us  [the longest x1 12.3 us: local(): blocks = lax.all_to_all(copies(blocks, npl), 'p', 0, 0)]
    all_to_all x4 -> x3, starting transfers between devices: 35.9 us -> 24.9 us  [the longest x1 10.6 us: local(): got = lax.all_to_all(chosen, 'z', 0, 0).reshape(nz, wanted, sub, 128)]
    dot_general x7 -> x0, matrix products: 7.17 us -> none  [times_t(): return lax.dot_general(a, b, ROWS, precision=lax.Precision.HIGHEST)]
    pallas_call x1 -> x2, Pallas kernels: 14.5 us -> 19.6 us  [call(): pl.pallas_call(kernel, in_specs=specs, out_specs=[pl.BlockSpec(memory_spa...]
    unnamed x12 -> x14, local copies, waits for them, and re-layouts: 2.08 us -> 3.38 us
    broadcast_in_dim x6 -> x4, local copies, waits for them, and re-layouts: 2.78 us -> 2.12 us  [copies(): return jnp.broadcast_to(x[None], (count,) + x.shape)]
  transfers between devices with their start and end apart: 5 -> 4, of which waited for: 4 -> 3; matrix products, arithmetic and copies ran while one was open for 4% -> 0% of each run, Pallas kernels for 11% -> 13%
where the time goes in v3:
time: 121 us
  starting transfers between devices  35.1 us (29%)
  waiting for transfers between devices  29.3 us (24%)
  blocking collectives  24 us (20%)
  Pallas kernels  19.6 us (16%)
  local copies, waits for them, and re-layouts  6.89 us (6%)
  between operations  5.65 us (5%)
    all_to_all x1, blocking collectives, local(): held = lax.all_to_all(copies(jnp.concatenate(held), nz), 'z', 0, 0)  24 us
    pallas_call x2, Pallas kernels, call(): pl.pallas_call(kernel, in_specs=specs, out_specs=[pl.BlockSpec(memory_spa...  19.6 us
    all_to_all x1, waiting for transfers between devices, local(): blocks = lax.all_to_all(copies(blocks, npl), 'p', 0, 0)  12.3 us
    all_to_all x1, waiting for transfers between devices, local(): got = lax.all_to_all(chosen, 'z', 0, 0).reshape(nz, wanted, sub, 128)  11.7 us
    all_to_all x1, starting transfers between devices, local(): got = lax.all_to_all(chosen, 'z', 0, 0).reshape(nz, wanted, sub, 128)  10.6 us
    all_to_all x1, starting transfers between devices, local(): pieces = lax.all_to_all(own.reshape(npl, coarse, width), 'p', 0, 0)  10.3 us
    all_to_all x1, starting transfers between devices, local(): blocks = lax.all_to_all(copies(blocks, npl), 'p', 0, 0)  9.8 us
    all_to_all x1, waiting for transfers between devices, local(): pieces = lax.all_to_all(own.reshape(npl, coarse, width), 'p', 0, 0)  5.26 us
  transfers between devices with their start and end apart: 4, of which 3 were waited for; matrix products, arithmetic and copies ran while one was open for 0% of the time, Pallas kernels for 13%

profile of v3, /device:TPU:1, one launch (start us, length us, event | category | flops | bytes accessed | tf_op | source)
XLA Modules:
  0.0 120.6 jit_solution(4354865200829740044)
XLA Ops:
  0.6 0.0 copy-start.1
  0.6 10.3 %all-to-all-start = ((f32[8,32,512]{2,1,0:T(8,128)}), f32[8,32,512]{2,1,0:T(8,128)S(1)}, u32[]{:S(2)}, u32[]{:S(2)}) async-start(f32[8,32,512]{2,1,0:T(8,128)} %bitcast.30), calls=%async_computation | async-start | bytes 1048576 | tf_op jit(solution)/shard_map/all_to_all | solution.py:207
  10.9 0.0 copy-done.1
  10.9 0.6 fusion.1
  15.2 5.3 %all-to-all-done = f32[8,32,512]{2,1,0:T(8,128)S(1)} async-done(((f32[8,32,512]{2,1,0:T(8,128)}), f32[8,32,512]{2,1,0:T(8,128)S(1)}, u32[]{:S(2)}, u32[]{:S(2)}) %all-to-all-start) | async-done | bytes 524320 | tf_op jit(solution)/shard_map/all_to_all | solution.py:207
  20.5 0.7 copy.6
  21.2 10.6 %all-to-all-start.1 = ((f32[16,32,128]{2,1,0:T(8,128)}), f32[16,32,128]{2,1,0:T(8,128)S(1)}, u32[]{:S(2)}, u32[]{:S(2)}) async-start(f32[16,32,128]{2,1,0:T(8,128)} %bitcast.6), calls=%async_computation.1 | async-start | bytes 524288 | tf_op jit(solution)/shard_map/all_to_all | solution.py:213
  33.1 11.7 %all-to-all-done.1 = f32[16,32,128]{2,1,0:T(8,128)S(1)} async-done(((f32[16,32,128]{2,1,0:T(8,128)}), f32[16,32,128]{2,1,0:T(8,128)S(1)}, u32[]{:S(2)}, u32[]{:S(2)}) %all-to-all-start.1) | async-done | bytes 262176 | tf_op jit(solution)/shard_map/all_to_all | solution.py:213
  44.9 24.0 %all_to_all.25 = f32[16,32,128]{2,1,0:T(8,128)S(1)} all-to-all(f32[16,32,128]{2,1,0:T(8,128)S(1)} %broadcast_in_dim.30), channel_id=1, replica_groups=mesh['z'=16,'p'=8,'x'=4] {'z'}, dimensions={0} | all-to-all | bytes 524288 | tf_op jit(solution)/shard_map/all_to_all | solution.py:216
  68.9 1.0 broadcast_in_dim.31
  69.9 9.8 %all-to-all-start.3 = ((f32[8,3,32,256]{3,2,1,0:T(8,128)}), f32[8,3,32,256]{3,2,1,0:T(8,128)S(1)}, u32[]{:S(2)}, u32[]{:S(2)}) async-start(f32[8,3,32,256]{3,2,1,0:T(8,128)} %broadcast_in_dim.31), calls=%async_computation.3 | async-start | bytes 1572864 | tf_op jit(solution)/shard_map/all_to_all | solution.py:220
  79.7 12.3 %all-to-all-done.3.blocks = f32[8,3,32,256]{3,2,1,0:T(8,128)S(1)} async-done(((f32[8,3,32,256]{3,2,1,0:T(8,128)}), f32[8,3,32,256]{3,2,1,0:T(8,128)S(1)}, u32[]{:S(2)}, u32[]{:S(2)}) %all-to-all-start.3) | async-done | bytes 786464 | tf_op jit(solution)/shard_map/all_to_all | solution.py:220
  92.0 1.1 broadcast_in_dim.34
  93.1 0.0 copy-start
  93.1 4.5 %all-to-all-start.4 = ((f32[8,2,32,512]{3,2,1,0:T(8,128)}), f32[8,2,32,512]{3,2,1,0:T(8,128)S(1)}, u32[]{:S(2)}, u32[]{:S(2)}) async-start(f32[8,2,32,512]{3,2,1,0:T(8,128)} %broadcast_in_dim.34), calls=%async_computation.4 | async-start | bytes 2097152 | tf_op jit(solution)/shard_map/all_to_all | solution.py:221
  97.6 0.0 copy-start.3
  97.6 0.0 copy-done
  97.6 0.7 copy-done.3
  98.3 0.0 copy-start.2
  98.3 16.1 %shard_map.59 = (f32[256,256]{1,0:T(8,128)S(1)}, f32[256,256]{1,0:T(8,128)S(1)}, f32[256,256]{1,0:T(8,128)S(1)}, f32[256,512]{1,0:T(8,128)}) custom-call(s32[1]{0:T(128)} %bitcast.row_ref, s32[2,128]{1,0:T(2,128)S(1)} %copy-done.3, f32[8,3,32,256]{3,2,1,0:T(8,128)S(1)} %all-to-all-done.3.blocks, f32[256,512]{1,0:T(8,128)S(1)} %bitcast.31), custom_call_target="tpu_custom_call" | custom-call | flops 17179869184 | bytes 1048576 | tf_op jit(solution)/shard_map/pallas_call | solution.py:180
  114.4 0.0 copy-start.5
  114.4 0.7 copy-done.5
  115.1 0.0 all-to-all-done.4.targets
  115.1 0.0 copy-done.2
  115.1 0.0 copy-start.4
  115.1 1.0 copy-done.4
  116.2 0.0 copy-start.6
  116.2 0.9 copy-done.6
  117.1 3.5 %shard_map.60 = f32[256,512]{1,0:T(8,128)} custom-call(s32[1]{0:T(128)} %bitcast.row_ref, s32[2,128]{1,0:T(2,128)S(1)} %copy-done.3, s32[2]{0:T(128)S(1)} %copy-done.1, f32[8,2,32,512]{3,2,1,0:T(8,128)S(1)} %all-to-all-done.4.targets, f32[256,256]{1,0:T(8,128)S(1)} %get-tuple-element.7.lead, f32[256,256]{1,0:T(8,128)S(1)} %get-tuple-element.8.below, ...), custom_call_target="tpu_custom_call" | custom-call | flops 1073741824 | bytes 1048576 | tf_op jit(solution)/shard_map/pallas_call | solution.py:180
  (13 shorter events, 0.1 us)
Async XLA Ops:
  0.6 10.3 %copy-start.1 = (s32[2]{0:T(128)S(1)}, s32[2]{0:T(128)}, u32[]{:S(2)}) copy-start(s32[2]{0:T(128)} %rows.1) | copy-start | bytes 28
  0.6 19.8 %all-to-all-start = ((f32[8,32,512]{2,1,0:T(8,128)}), f32[8,32,512]{2,1,0:T(8,128)S(1)}, u32[]{:S(2)}, u32[]{:S(2)}) async-start(f32[8,32,512]{2,1,0:T(8,128)} %bitcast.30), calls=%async_computation | async-start | bytes 1048576 | tf_op jit(solution)/shard_map/all_to_all | solution.py:207
  21.2 23.6 %all-to-all-start.1 = ((f32[16,32,128]{2,1,0:T(8,128)}), f32[16,32,128]{2,1,0:T(8,128)S(1)}, u32[]{:S(2)}, u32[]{:S(2)}) async-start(f32[16,32,128]{2,1,0:T(8,128)} %bitcast.6), calls=%async_computation.1 | async-start | bytes 524288 | tf_op jit(solution)/shard_map/all_to_all | solution.py:213
  69.9 22.1 %all-to-all-start.3 = ((f32[8,3,32,256]{3,2,1,0:T(8,128)}), f32[8,3,32,256]{3,2,1,0:T(8,128)S(1)}, u32[]{:S(2)}, u32[]{:S(2)}) async-start(f32[8,3,32,256]{3,2,1,0:T(8,128)} %broadcast_in_dim.31), calls=%async_computation.3 | async-start | bytes 1572864 | tf_op jit(solution)/shard_map/all_to_all | solution.py:220
  93.1 4.5 %copy-start = (f32[1,256,512]{2,1,0:T(8,128)S(1)}, f32[1,256,512]{2,1,0:T(8,128)}, u32[]{:S(2)}) copy-start(f32[1,256,512]{2,1,0:T(8,128)} %param.4) | copy-start | bytes 1572868
  93.1 22.0 %all-to-all-start.4 = ((f32[8,2,32,512]{3,2,1,0:T(8,128)}), f32[8,2,32,512]{3,2,1,0:T(8,128)S(1)}, u32[]{:S(2)}, u32[]{:S(2)}) async-start(f32[8,2,32,512]{3,2,1,0:T(8,128)} %broadcast_in_dim.34), calls=%async_computation.4 | async-start | bytes 2097152 | tf_op jit(solution)/shard_map/all_to_all | solution.py:221
  97.6 0.7 copy-start.3
  98.3 16.9 %copy-start.2 = (f32[1,256,512]{2,1,0:T(8,128)S(1)}, f32[1,256,512]{2,1,0:T(8,128)}, u32[]{:S(2)}) copy-start(f32[1,256,512]{2,1,0:T(8,128)} %param.5) | copy-start | bytes 1572868
  114.4 0.7 copy-start.5
  115.1 1.0 copy-start.4
  116.2 0.9 copy-start.6

commit v4 on v3

--- a/solution.py
+++ b/solution.py
@@ -135,19 +135,21 @@
     return pattern[part, row].astype(jnp.float32)
 
 
-def pivot_kernel(row_ref, pattern, blocks, own, lead, below, second, mine):
+def pivot_kernel(blocks, solver):
+    size, half = solver.shape[1:]
+    w00 = inverse_factor(blocks[:, 0].reshape(size, half))
+    solver[0] = w00
+    l10 = dot6(split(blocks[:, 1].reshape(size, half)), split(w00))
+    solver[1] = l10
+    l10 = split(l10)
+    solver[2] = inverse_factor(blocks[:, 2].reshape(size, half) - dot6(l10, l10))
+
+
+def own_kernel(row_ref, pattern, own, solver, mine):
     size, width = own.shape
     half = width // 2
     row = row_ref[0]
-    w00 = inverse_factor(blocks[:, 0].reshape(size, half))
-    lead[...] = w00
-    w00 = split(w00)
-    l10 = dot6(split(blocks[:, 1].reshape(size, half)), w00)
-    below[...] = l10
-    l10 = split(l10)
-    w11 = inverse_factor(blocks[:, 2].reshape(size, half) - dot6(l10, l10))
-    second[...] = w11
-    w11 = split(w11)
+    w00, l10, w11 = split(solver[0]), split(solver[1]), split(solver[2])
     one = dot6(split(own[:, :half] * flag(pattern, 0, row)), w00)
     inner = own[:, half:] * flag(pattern, 1, row) - dot6(split(one), l10)
     two = dot6(split(inner), w11)
@@ -157,10 +159,10 @@
     mine[:, half:] = jnp.where((upper & (row == 1)) | (row == 0), 0.0, two)
 
 
-def update_kernel(row_ref, pattern, rows, targets, lead, below, second, mine, trailing, out):
+def update_kernel(row_ref, pattern, rows, targets, solver, mine, trailing, out):
     size, width = mine.shape
     half = width // 2
-    w00, l10, w11 = split(lead[...]), split(below[...]), split(second[...])
+    w00, l10, w11 = split(solver[0]), split(solver[1]), split(solver[2])
     left, right = split(mine[:, :half]), split(mine[:, half:])
     keep = (row_ref[0] >= 2).astype(jnp.float32)
     for t in range(targets.shape[1]):
@@ -173,16 +175,15 @@
         out[:, at] = trailing[:, at] - keep * update
 
 
-def call(kernel, scalars, arrays, shapes, flops):
+def call(kernel, scalars, arrays, shape, flops, vmem=12):
     specs = [pl.BlockSpec(memory_space=pltpu.SMEM)] * len(scalars)
     specs += [pl.BlockSpec(memory_space=pltpu.VMEM)] * len(arrays)
-    outs = [jax.ShapeDtypeStruct(shape, jnp.float32) for shape in shapes]
     return pl.pallas_call(
         kernel,
         in_specs=specs,
-        out_specs=[pl.BlockSpec(memory_space=pltpu.VMEM)] * len(outs),
-        out_shape=outs,
-        compiler_params=pltpu.CompilerParams(vmem_limit_bytes=32 << 20),
+        out_specs=pl.BlockSpec(memory_space=pltpu.VMEM),
+        out_shape=jax.ShapeDtypeStruct(shape, jnp.float32),
+        compiler_params=pltpu.CompilerParams(vmem_limit_bytes=vmem << 20),
         cost_estimate=pl.CostEstimate(flops=flops, bytes_accessed=1 << 20, transcendentals=0),
     )(*scalars, *arrays)
 
@@ -198,40 +199,37 @@
 def local(panel, trailing, pattern, target_rows):
     _, size, width = panel.shape
     half = width // 2
-    nz, npl = lax.axis_size("z"), lax.axis_size("p")
+    nz, npl, nx = lax.axis_size("z"), lax.axis_size("p"), lax.axis_size("x")
     row = (lax.axis_index("z") * npl + lax.axis_index("p")).astype(jnp.int32)[None]
     count = target_rows.shape[0]
     own = panel[0]
-    coarse, lanes = size // npl, width // 128
-    sub = coarse * lanes // nz
-    pieces = lax.all_to_all(own.reshape(npl, coarse, width), "p", 0, 0)
-    chosen = [pieces[0], pieces[1]]
-    chosen += [pick(pieces, target_rows[t] % npl, 0) for t in range(count)]
-    wanted = len(chosen)
-    chosen = jnp.stack(chosen).reshape(wanted, coarse // sub, sub, lanes, 128)
-    chosen = chosen.transpose(1, 3, 0, 2, 4).reshape(nz, wanted * sub, 128)
-    got = lax.all_to_all(chosen, "z", 0, 0).reshape(nz, wanted, sub, 128)
-    held = [got[0, 0], got[0, 1]]
-    held += [pick(got[:, 2 + t], target_rows[t] // npl, 0) for t in range(count)]
-    held = lax.all_to_all(copies(jnp.concatenate(held), nz), "z", 0, 0)
-    held = held.reshape(coarse // sub, lanes, wanted, sub, 128).transpose(2, 0, 3, 1, 4)
-    held = held.reshape(wanted, coarse, width)
+    fine, lanes = size // (npl * nx), width // 128
+    sub = fine * lanes // nz
+    shares = npl * nx
+    everyone = lax.all_gather(target_rows, "x", axis=0, tiled=True)
+    pieces = pick(own.reshape(npl, nx, fine, width), lax.axis_index("x"), 1)
+    pieces = pieces.reshape(npl, fine // sub, sub, lanes, 128).transpose(1, 3, 0, 2, 4)
+    pieces = lax.all_to_all(pieces.reshape(nz * npl, sub, 128), ("z", "p"), 0, 0)
+    held = jnp.concatenate(
+        [pieces[:2]]
+        + [lax.dynamic_slice_in_dim(pieces, everyone[t], 1, 0) for t in range(count * nx)]
+    )
+    wanted = held.shape[0]
+    held = lax.all_to_all(copies(held.reshape(wanted * sub, 128), nz), "z", 0, 0)
+    held = held.reshape(fine // sub, lanes, wanted, sub, 128).transpose(2, 0, 3, 1, 4)
+    held = held.reshape(wanted, fine, width)
     blocks = jnp.stack([held[0, :, :half], held[1, :, :half], held[1, :, half:]])
-    blocks = lax.all_to_all(copies(blocks, npl), "p", 0, 0)
-    targets = lax.all_to_all(copies(held[2:], npl), "p", 0, 0)
-    square = (size, half)
-    lead, below, second, mine = call(
-        pivot_kernel,
-        (row, pattern),
-        (blocks, own),
-        (square, square, square, (size, width)),
-        1 << 34,
-    )
-    (schur,) = call(
+    blocks = lax.all_to_all(copies(blocks, shares), ("p", "x"), 0, 0)
+    targets = copies(held[2:].reshape(nx, count, fine, width), npl)
+    targets = targets.reshape(shares, count, fine, width)
+    targets = lax.all_to_all(targets, ("p", "x"), 0, 0)
+    solver = call(pivot_kernel, (), (blocks,), (3, size, half), 1 << 34, 16)
+    mine = call(own_kernel, (row, pattern), (own, solver), (size, width), 1 << 30)
+    schur = call(
         update_kernel,
         (row, pattern, target_rows),
-        (targets, lead, below, second, mine, trailing[0]),
-        ((size, trailing.shape[2]),),
+        (targets, solver, mine, trailing[0]),
+        (size, trailing.shape[2]),
         1 << 30,
     )
     return mine[None], schur[None]

time: 121 us -> 127 us (1.050)
  waiting for transfers between devices: 29.3 us -> 13.6 us
  between operations: 5.65 us -> 16.4 us
  blocking collectives: 24 us -> 31.1 us
  local copies, waits for them, and re-layouts: 6.89 us -> 8.67 us
    all_to_all x4 -> x3, waiting for transfers between devices: 29.3 us -> 13.6 us  [the longest x1 13.6 us: local(): blocks = lax.all_to_all(copies(blocks, shares), ('p', 'x'), 0, 0)]
    unnamed x0 -> x1, blocking collectives: none -> 7.45 us
    unnamed x14 -> x22, local copies, waits for them, and re-layouts: 3.38 us -> 4.84 us
    all_to_all x4 -> x3, starting transfers between devices: 35.1 us -> 36.1 us  [the longest x1 20.6 us: local(): lax.all_to_all(pieces.reshape(nz * npl, sub, 128), ('z', 'p'), 0, 0)]
    pallas_call x2 -> x3, Pallas kernels: 19.6 us -> 20.5 us  [call(): pl.pallas_call(kernel, in_specs=specs, out_specs=pl.BlockSpec(memory_spac...]
  transfers between devices with their start and end apart: 4 -> 3, of which waited for: 3 -> 1; matrix products, arithmetic and copies ran while one was open for 0% -> 2% of each run, Pallas kernels for 13% -> 13%
where the time goes in v4:
time: 127 us; the launch traced here: 126 us
  starting transfers between devices  36.1 us (28%)
  blocking collectives  31.1 us (24%)
  Pallas kernels  20.5 us (16%)
  between operations  16.4 us (13%)
  waiting for transfers between devices  13.6 us (11%)
  local copies, waits for them, and re-layouts  8.67 us (7%)
    all_to_all x1, blocking collectives, local(): lax.all_to_all(copies(held.reshape(wanted * sub, 128), nz), 'z', 0, 0)  23.6 us
    all_to_all x1, starting transfers between devices, local(): lax.all_to_all(pieces.reshape(nz * npl, sub, 128), ('z', 'p'), 0, 0)  20.6 us
    pallas_call x3, Pallas kernels, call(): pl.pallas_call(kernel, in_specs=specs, out_specs=pl.BlockSpec(memory_spac...  20.5 us
    all_to_all x1, waiting for transfers between devices, local(): blocks = lax.all_to_all(copies(blocks, shares), ('p', 'x'), 0, 0)  13.6 us
    all_to_all x1, starting transfers between devices, local(): blocks = lax.all_to_all(copies(blocks, shares), ('p', 'x'), 0, 0)  10.6 us
    unnamed x1, blocking collectives  7.45 us
    all_to_all x1, starting transfers between devices, local(): targets = lax.all_to_all(targets, ('p', 'x'), 0, 0)  4.96 us
    unnamed x22, local copies, waits for them, and re-layouts  4.84 us
  transfers between devices with their start and end apart: 3, of which 1 were waited for; matrix products, arithmetic and copies ran while one was open for 2% of the time, Pallas kernels for 13%

profile of v4, /device:TPU:1, one launch (start us, length us, event | category | flops | bytes accessed | tf_op | source)
XLA Modules:
  0.0 126.4 jit_solution(16456694162695869130)
XLA Ops:
  0.6 0.9 dynamic-slice_bitcast_fusion
  1.6 0.1 copy.12
  1.7 0.8 copy.13
  2.5 20.6 %all-to-all-start = ((f32[128,2,128]{2,1,0:T(2,128)}), f32[128,2,128]{2,1,0:T(2,128)S(1)}, u32[]{:S(2)}, u32[]{:S(2)}) async-start(f32[128,2,128]{2,1,0:T(2,128)} %copy.13), calls=%async_computation | async-start | bytes 262144 | tf_op jit(solution)/shard_map/all_to_all | solution.py:212
  23.0 1.3 %dynamic-slice = u32[1]{0:T(128)} dynamic-slice(u32[512]{0:T(512)} %constant.29, u32[]{:T(128)S(6)} %add.41), dynamic_slice_sizes={1} | dynamic-slice | bytes 12
  25.0 0.0 copy-start.3
  25.0 0.6 copy-done.3
  25.6 0.2 dynamic-update-slice
  25.8 7.4 %all-reduce = s32[8]{0:T(128)S(1)} all-reduce(s32[8]{0:T(128)S(1)} %dynamic-update-slice), channel_id=1, replica_groups=mesh['z'=16,'p'=8,'x'=4] {'x'}, use_global_device_ids=true, to_apply=%add | all-reduce | flops 8 | bytes 64
  33.2 0.7 fusion
  48.8 0.0 all-to-all-done
  49.0 23.6 %all_to_all.20 = f32[16,20,128]{2,1,0:T(8,128)S(1)} all-to-all(f32[16,20,128]{2,1,0:T(8,128)S(1)} %broadcast_in_dim.31), channel_id=1, replica_groups=mesh['z'=16,'p'=8,'x'=4] {'z'}, dimensions={0} | all-to-all | bytes 327680 | tf_op jit(solution)/shard_map/all_to_all | solution.py:218
  72.7 0.1 reshape.28
  72.9 0.9 broadcast_in_dim.32
  73.8 10.6 %all-to-all-start.2 = ((f32[32,3,8,256]{3,2,1,0:T(8,128)}), f32[32,3,8,256]{3,2,1,0:T(8,128)S(1)}, u32[]{:S(2)}, u32[]{:S(2)}) async-start(f32[32,3,8,256]{3,2,1,0:T(8,128)} %broadcast_in_dim.32), calls=%async_computation.2 | async-start | bytes 1572864 | tf_op jit(solution)/shard_map/all_to_all | solution.py:222
  84.4 0.1 broadcast_in_dim.34
  84.5 13.6 %all-to-all-done.2.blocks = f32[32,3,8,256]{3,2,1,0:T(8,128)S(1)} async-done(((f32[32,3,8,256]{3,2,1,0:T(8,128)}), f32[32,3,8,256]{3,2,1,0:T(8,128)S(1)}, u32[]{:S(2)}, u32[]{:S(2)}) %all-to-all-start.2) | async-done | bytes 786464 | tf_op jit(solution)/shard_map/all_to_all | solution.py:222
  98.0 1.1 broadcast_in_dim.35
  99.1 5.0 %all-to-all-start.3 = ((f32[32,2,8,512]{3,2,1,0:T(8,128)}), f32[32,2,8,512]{3,2,1,0:T(8,128)S(1)}, u32[]{:S(2)}, u32[]{:S(2)}) async-start(f32[32,2,8,512]{3,2,1,0:T(8,128)} %bitcast.18), calls=%async_computation.3 | async-start | bytes 2097152 | tf_op jit(solution)/shard_map/all_to_all | solution.py:225
  104.1 0.0 copy-start
  104.1 14.3 %shard_map.59.solver = f32[3,256,256]{2,1,0:T(8,128)S(1)} custom-call(f32[32,3,8,256]{3,2,1,0:T(8,128)S(1)} %all-to-all-done.2.blocks), custom_call_target="tpu_custom_call" | custom-call | flops 17179869184 | bytes 1048576 | tf_op jit(solution)/shard_map/pallas_call | solution.py:181
  118.4 0.0 copy-start.2
  118.4 0.0 copy-done
  118.5 0.7 copy-done.2
  119.1 0.0 copy-start.1
  119.1 2.7 %shard_map.60.mine = f32[256,512]{1,0:T(8,128)} custom-call(s32[1]{0:T(128)} %bitcast.row_ref, s32[2,128]{1,0:T(2,128)S(1)} %copy-done.2, f32[256,512]{1,0:T(8,128)S(1)} %bitcast.28, f32[3,256,256]{2,1,0:T(8,128)S(1)} %shard_map.59.solver), custom_call_target="tpu_custom_call" | custom-call | flops 1073741824 | bytes 1048576 | tf_op jit(solution)/shard_map/pallas_call | solution.py:181
  121.8 0.0 all-to-all-done.3.targets
  121.8 0.0 copy-done.1
  121.8 0.0 copy-start.4
  121.8 1.0 copy-done.4
  122.8 3.5 %shard_map.61 = f32[256,512]{1,0:T(8,128)} custom-call(s32[1]{0:T(128)} %bitcast.row_ref, s32[2,128]{1,0:T(2,128)S(1)} %copy-done.2, s32[2]{0:T(128)S(1)} %copy-done.3, f32[32,2,8,512]{3,2,1,0:T(8,128)S(1)} %all-to-all-done.3.targets, f32[3,256,256]{2,1,0:T(8,128)S(1)} %shard_map.59.solver, f32[256,512]{1,0:T(8,128)S(1)} %copy-done.4, f32[256,512]{1,0:T(8,128)S(1)} %bitcast.29), custom_call_target="tpu_custom_call" | custom-call | flops 1073741824 | bytes 1048576 | tf_op jit(solution)/shard_map/pallas_call | solution.py:181
  (20 shorter events, 0.3 us)
Async XLA Ops:
  2.5 46.4 %all-to-all-start = ((f32[128,2,128]{2,1,0:T(2,128)}), f32[128,2,128]{2,1,0:T(2,128)S(1)}, u32[]{:S(2)}, u32[]{:S(2)}) async-start(f32[128,2,128]{2,1,0:T(2,128)} %copy.13), calls=%async_computation | async-start | bytes 262144 | tf_op jit(solution)/shard_map/all_to_all | solution.py:212
  25.0 0.7 copy-start.3
  73.8 24.2 %all-to-all-start.2 = ((f32[32,3,8,256]{3,2,1,0:T(8,128)}), f32[32,3,8,256]{3,2,1,0:T(8,128)S(1)}, u32[]{:S(2)}, u32[]{:S(2)}) async-start(f32[32,3,8,256]{3,2,1,0:T(8,128)} %broadcast_in_dim.32), calls=%async_computation.2 | async-start | bytes 1572864 | tf_op jit(solution)/shard_map/all_to_all | solution.py:222
  99.1 22.7 %all-to-all-start.3 = ((f32[32,2,8,512]{3,2,1,0:T(8,128)}), f32[32,2,8,512]{3,2,1,0:T(8,128)S(1)}, u32[]{:S(2)}, u32[]{:S(2)}) async-start(f32[32,2,8,512]{3,2,1,0:T(8,128)} %bitcast.18), calls=%async_computation.3 | async-start | bytes 2097152 | tf_op jit(solution)/shard_map/all_to_all | solution.py:225
  104.1 14.3 %copy-start = (f32[1,256,512]{2,1,0:T(8,128)S(1)}, f32[1,256,512]{2,1,0:T(8,128)}, u32[]{:S(2)}) copy-start(f32[1,256,512]{2,1,0:T(8,128)} %param.4) | copy-start | bytes 1572868
  118.4 0.7 copy-start.2
  119.1 2.7 %copy-start.1 = (f32[1,256,512]{2,1,0:T(8,128)S(1)}, f32[1,256,512]{2,1,0:T(8,128)}, u32[]{:S(2)}) copy-start(f32[1,256,512]{2,1,0:T(8,128)} %param.5) | copy-start | bytes 1572868
  121.8 1.0 copy-start.4

commit v5 on v4

--- a/solution.py
+++ b/solution.py
@@ -203,27 +203,25 @@
     row = (lax.axis_index("z") * npl + lax.axis_index("p")).astype(jnp.int32)[None]
     count = target_rows.shape[0]
     own = panel[0]
-    fine, lanes = size // (npl * nx), width // 128
-    sub = fine * lanes // nz
-    shares = npl * nx
-    everyone = lax.all_gather(target_rows, "x", axis=0, tiled=True)
-    pieces = pick(own.reshape(npl, nx, fine, width), lax.axis_index("x"), 1)
-    pieces = pieces.reshape(npl, fine // sub, sub, lanes, 128).transpose(1, 3, 0, 2, 4)
-    pieces = lax.all_to_all(pieces.reshape(nz * npl, sub, 128), ("z", "p"), 0, 0)
+    fine, coarse = size // (npl * nx), size // npl
+    pieces = lax.all_to_all(own.reshape(npl, coarse, width), "p", 0, 0)
+    chosen = jnp.stack([pick(pieces, target_rows[t] % npl, 0) for t in range(count)])
+    chosen, pieces = lax.optimization_barrier((chosen, pieces))
+    planes = lax.all_gather(chosen, "z", axis=0)
+    share = lax.dynamic_slice_in_dim(pieces[:2], lax.axis_index("x") * fine, fine, 1)
+    share = jnp.stack([share[0, :, :half], share[1, :, :half], share[1, :, half:]])
+    share = lax.all_to_all(copies(share, nz), "z", 0, 0)[0]
+    blocks = lax.all_to_all(copies(share, npl * nx), ("p", "x"), 0, 0)
+    solver = call(pivot_kernel, (), (blocks,), (3, size, half), 1 << 34, 16)
+    planes, solver = lax.optimization_barrier((planes, solver))
     held = jnp.concatenate(
-        [pieces[:2]]
-        + [lax.dynamic_slice_in_dim(pieces, everyone[t], 1, 0) for t in range(count * nx)]
-    )
-    wanted = held.shape[0]
-    held = lax.all_to_all(copies(held.reshape(wanted * sub, 128), nz), "z", 0, 0)
-    held = held.reshape(fine // sub, lanes, wanted, sub, 128).transpose(2, 0, 3, 1, 4)
-    held = held.reshape(wanted, fine, width)
-    blocks = jnp.stack([held[0, :, :half], held[1, :, :half], held[1, :, half:]])
-    blocks = lax.all_to_all(copies(blocks, shares), ("p", "x"), 0, 0)
-    targets = copies(held[2:].reshape(nx, count, fine, width), npl)
-    targets = targets.reshape(shares, count, fine, width)
-    targets = lax.all_to_all(targets, ("p", "x"), 0, 0)
-    solver = call(pivot_kernel, (), (blocks,), (3, size, half), 1 << 34, 16)
+        [
+            lax.dynamic_slice(planes, (target_rows[t] // npl, t, 0, 0), (1, 1, coarse, width))
+            for t in range(count)
+        ],
+        axis=1,
+    )[0]
+    targets = lax.all_to_all(copies(held, npl), "p", 0, 0)
     mine = call(own_kernel, (row, pattern), (own, solver), (size, width), 1 << 30)
     schur = call(
         update_kernel,

time: 127 us -> 150 us (1.18)
  waiting for transfers between devices: 13.6 us -> 56.8 us
  blocking collectives: 31.1 us -> 0 us
  starting transfers between devices: 36.1 us -> 46.2 us
  local copies, waits for them, and re-layouts: 8.67 us -> 6.1 us
  between operations: 16.4 us -> 18.7 us
    all_to_all x3 -> x4, waiting for transfers between devices: 13.6 us -> 47 us  [the longest x1 17.3 us: local(): share = lax.all_to_all(copies(share, nz), 'z', 0, 0)[0]]
    all_to_all x1 -> x0, blocking collectives: 23.6 us -> none  [local(): lax.all_to_all(copies(held.reshape(wanted * sub, 128), nz), 'z', 0, 0)]
    all_to_all x3 -> x4, starting transfers between devices: 36.1 us -> 46.2 us  [the longest x1 13.9 us: local(): targets = lax.all_to_all(copies(held, npl), 'p', 0, 0)]
    all_gather x0 -> x1, waiting for transfers between devices: none -> 9.07 us  [local(): planes = lax.all_gather(chosen, 'z', axis=0)]
    unnamed x1 -> x0, blocking collectives: 7.45 us -> none
    unnamed x22 -> x10, local copies, waits for them, and re-layouts: 4.84 us -> 1.06 us
  transfers between devices with their start and end apart: 3 -> 5, of which waited for: 1 -> 5; matrix products, arithmetic and copies ran while one was open for 2% -> 1% of each run, Pallas kernels for 13% -> 11%
where the time goes in v5:
time: 150 us; the launch traced here: 149 us
  waiting for transfers between devices  56.8 us (38%)
  starting transfers between devices  46.2 us (31%)
  Pallas kernels  20.5 us (14%)
  between operations  18.7 us (12%)
  local copies, waits for them, and re-layouts  6.1 us (4%)
    pallas_call x3, Pallas kernels, call(): pl.pallas_call(kernel, in_specs=specs, out_specs=pl.BlockSpec(memory_spac...  20.5 us
    all_to_all x1, waiting for transfers between devices, local(): share = lax.all_to_all(copies(share, nz), 'z', 0, 0)[0]  17.3 us
    all_to_all x1, starting transfers between devices, local(): targets = lax.all_to_all(copies(held, npl), 'p', 0, 0)  13.9 us
    all_to_all x1, waiting for transfers between devices, local(): blocks = lax.all_to_all(copies(share, npl * nx), ('p', 'x'), 0, 0)  12.5 us
    all_to_all x1, waiting for transfers between devices, local(): targets = lax.all_to_all(copies(held, npl), 'p', 0, 0)  12.4 us
    all_to_all x1, starting transfers between devices, local(): blocks = lax.all_to_all(copies(share, npl * nx), ('p', 'x'), 0, 0)  11.4 us
    all_to_all x1, starting transfers between devices, local(): share = lax.all_to_all(copies(share, nz), 'z', 0, 0)[0]  10.6 us
    all_to_all x1, starting transfers between devices, local(): pieces = lax.all_to_all(own.reshape(npl, coarse, width), 'p', 0, 0)  10.3 us
  transfers between devices with their start and end apart: 5, of which 5 were waited for; matrix products, arithmetic and copies ran while one was open for 1% of the time, Pallas kernels for 11%

profile of v5, /device:TPU:1, one launch (start us, length us, event | category | flops | bytes accessed | tf_op | source)
XLA Modules:
  0.0 149.0 jit_solution(11095473062379930717)
XLA Ops:
  7.2 10.3 %all-to-all-start = ((f32[8,32,512]{2,1,0:T(8,128)}), f32[8,32,512]{2,1,0:T(8,128)S(1)}, u32[]{:S(2)}, u32[]{:S(2)}) async-start(f32[8,32,512]{2,1,0:T(8,128)} %bitcast.13), calls=%async_computation | async-start | bytes 1048576 | tf_op jit(solution)/shard_map/all_to_all | solution.py:207
  17.4 1.3 fusion
  22.1 4.8 %all-to-all-done = f32[8,32,512]{2,1,0:T(8,128)S(1)} async-done(((f32[8,32,512]{2,1,0:T(8,128)}), f32[8,32,512]{2,1,0:T(8,128)S(1)}, u32[]{:S(2)}, u32[]{:S(2)}) %all-to-all-start) | async-done | bytes 524320 | tf_op jit(solution)/shard_map/all_to_all | solution.py:207
  27.0 0.7 pad_maximum_fusion
  27.7 0.8 broadcast_in_dim.30
  28.5 10.6 %all-to-all-start.1 = ((f32[16,3,8,256]{3,2,1,0:T(8,128)}), f32[16,3,8,256]{3,2,1,0:T(8,128)S(1)}, u32[]{:S(2)}, u32[]{:S(2)}) async-start(f32[16,3,8,256]{3,2,1,0:T(8,128)} %broadcast_in_dim.30), calls=%async_computation.1 | async-start | bytes 786432 | tf_op jit(solution)/shard_map/all_to_all | solution.py:213
  39.1 0.0 all-gather.3.cloned.1.call-start
  39.1 0.7 all-gather.3.cloned.1.call-update
  39.8 17.3 %all-to-all-done.1 = f32[16,3,8,256]{3,2,1,0:T(8,128)S(1)} async-done(((f32[16,3,8,256]{3,2,1,0:T(8,128)}), f32[16,3,8,256]{3,2,1,0:T(8,128)S(1)}, u32[]{:S(2)}, u32[]{:S(2)}) %all-to-all-start.1) | async-done | bytes 393248 | tf_op jit(solution)/shard_map/all_to_all | solution.py:213
  57.1 0.9 broadcast_in_dim.32
  58.1 11.4 %all-to-all-start.2 = ((f32[32,3,8,256]{3,2,1,0:T(8,128)}), f32[32,3,8,256]{3,2,1,0:T(8,128)S(1)}, u32[]{:S(2)}, u32[]{:S(2)}) async-start(f32[32,3,8,256]{3,2,1,0:T(8,128)} %broadcast_in_dim.32), calls=%async_computation.2 | async-start | bytes 1572864 | tf_op jit(solution)/shard_map/all_to_all | solution.py:214
  70.7 12.5 %all-to-all-done.2.blocks = f32[32,3,8,256]{3,2,1,0:T(8,128)S(1)} async-done(((f32[32,3,8,256]{3,2,1,0:T(8,128)}), f32[32,3,8,256]{3,2,1,0:T(8,128)S(1)}, u32[]{:S(2)}, u32[]{:S(2)}) %all-to-all-start.2) | async-done | bytes 786464 | tf_op jit(solution)/shard_map/all_to_all | solution.py:214
  83.2 14.3 %shard_map.59.solver = f32[3,256,256]{2,1,0:T(8,128)S(1)} custom-call(f32[32,3,8,256]{3,2,1,0:T(8,128)S(1)} %all-to-all-done.2.blocks), custom_call_target="tpu_custom_call" | custom-call | flops 17179869184 | bytes 1048576 | tf_op jit(solution)/shard_map/pallas_call | solution.py:181
  97.5 0.0 copy-start
  97.5 0.0 copy-start.3
  97.5 9.1 %all-gather.3.cloned.1.call-done = f32[32,32,512]{2,1,0:T(8,128)} async-done(((f32[2,32,512]{2,1,0:T(8,128)}), f32[32,32,512]{2,1,0:T(8,128)}) %all-gather.3.cloned.1.call-update) | async-done | bytes 2097168 | tf_op jit(solution)/shard_map/all_gather | solution.py:210
  106.6 0.9 constant_dynamic-slice_fusion.2
  107.5 1.1 broadcast_in_dim.35
  108.6 13.9 %all-to-all-start.3 = ((f32[8,2,32,512]{3,2,1,0:T(8,128)}), f32[8,2,32,512]{3,2,1,0:T(8,128)S(1)}, u32[]{:S(2)}, u32[]{:S(2)}) async-start(f32[8,2,32,512]{3,2,1,0:T(8,128)} %broadcast_in_dim.35), calls=%async_computation.3 | async-start | bytes 2097152 | tf_op jit(solution)/shard_map/all_to_all | solution.py:224
  122.5 0.0 copy-start.1
  122.5 0.0 copy-start.2
  122.5 0.0 copy-done
  122.5 0.0 copy-done.3
  122.5 2.7 %shard_map.60.mine = f32[256,512]{1,0:T(8,128)} custom-call(s32[1]{0:T(128)} %bitcast.row_ref, s32[2,128]{1,0:T(2,128)S(1)} %copy-done.3, f32[256,512]{1,0:T(8,128)S(1)} %bitcast.14, f32[3,256,256]{2,1,0:T(8,128)S(1)} %shard_map.59.solver), custom_call_target="tpu_custom_call" | custom-call | flops 1073741824 | bytes 1048576 | tf_op jit(solution)/shard_map/pallas_call | solution.py:181
  125.2 12.4 %all-to-all-done.3.targets = f32[8,2,32,512]{3,2,1,0:T(8,128)S(1)} async-done(((f32[8,2,32,512]{3,2,1,0:T(8,128)}), f32[8,2,32,512]{3,2,1,0:T(8,128)S(1)}, u32[]{:S(2)}, u32[]{:S(2)}) %all-to-all-start.3) | async-done | bytes 1048608 | tf_op jit(solution)/shard_map/all_to_all | solution.py:224
  137.6 0.0 copy-done.1
  137.6 0.0 copy-done.2
  137.6 0.0 copy-start.4
  137.6 1.0 copy-done.4
  138.6 3.5 %shard_map.61 = f32[256,512]{1,0:T(8,128)} custom-call(s32[1]{0:T(128)} %bitcast.row_ref, s32[2,128]{1,0:T(2,128)S(1)} %copy-done.3, s32[2]{0:T(128)S(1)} %copy-done.1, f32[8,2,32,512]{3,2,1,0:T(8,128)S(1)} %all-to-all-done.3.targets, f32[3,256,256]{2,1,0:T(8,128)S(1)} %shard_map.59.solver, f32[256,512]{1,0:T(8,128)S(1)} %copy-done.4, f32[256,512]{1,0:T(8,128)S(1)} %bitcast.15), custom_call_target="tpu_custom_call" | custom-call | flops 1073741824 | bytes 1048576 | tf_op jit(solution)/shard_map/pallas_call | solution.py:181
  (7 shorter events, 0.1 us)
Async XLA Ops:
  7.2 19.8 %all-to-all-start = ((f32[8,32,512]{2,1,0:T(8,128)}), f32[8,32,512]{2,1,0:T(8,128)S(1)}, u32[]{:S(2)}, u32[]{:S(2)}) async-start(f32[8,32,512]{2,1,0:T(8,128)} %bitcast.13), calls=%async_computation | async-start | bytes 1048576 | tf_op jit(solution)/shard_map/all_to_all | solution.py:207
  28.5 28.7 %all-to-all-start.1 = ((f32[16,3,8,256]{3,2,1,0:T(8,128)}), f32[16,3,8,256]{3,2,1,0:T(8,128)S(1)}, u32[]{:S(2)}, u32[]{:S(2)}) async-start(f32[16,3,8,256]{3,2,1,0:T(8,128)} %broadcast_in_dim.30), calls=%async_computation.1 | async-start | bytes 786432 | tf_op jit(solution)/shard_map/all_to_all | solution.py:213
  39.1 67.5 %all-gather.3.cloned.1.call-start = ((), (), s32[]{:S(2)}) async-start(), calls=%async_computation.4 | async-start | bytes 2228224 | tf_op jit(solution)/shard_map/all_gather | solution.py:210
  58.1 25.1 %all-to-all-start.2 = ((f32[32,3,8,256]{3,2,1,0:T(8,128)}), f32[32,3,8,256]{3,2,1,0:T(8,128)S(1)}, u32[]{:S(2)}, u32[]{:S(2)}) async-start(f32[32,3,8,256]{3,2,1,0:T(8,128)} %broadcast_in_dim.32), calls=%async_computation.2 | async-start | bytes 1572864 | tf_op jit(solution)/shard_map/all_to_all | solution.py:214
  97.5 25.0 %copy-start = (f32[1,256,512]{2,1,0:T(8,128)S(1)}, f32[1,256,512]{2,1,0:T(8,128)}, u32[]{:S(2)}) copy-start(f32[1,256,512]{2,1,0:T(8,128)} %param.4) | copy-start | bytes 1572868
  97.5 25.0 %copy-start.3 = (s32[2,128]{1,0:T(2,128)S(1)}, s32[2,128]{1,0:T(2,128)}, u32[]{:S(2)}) copy-start(s32[2,128]{1,0:T(2,128)} %pattern.3) | copy-start | bytes 3076
  108.6 29.0 %all-to-all-start.3 = ((f32[8,2,32,512]{3,2,1,0:T(8,128)}), f32[8,2,32,512]{3,2,1,0:T(8,128)S(1)}, u32[]{:S(2)}, u32[]{:S(2)}) async-start(f32[8,2,32,512]{3,2,1,0:T(8,128)} %broadcast_in_dim.35), calls=%async_computation.3 | async-start | bytes 2097152 | tf_op jit(solution)/shard_map/all_to_all | solution.py:224
  122.5 15.1 %copy-start.1 = (s32[2]{0:T(128)S(1)}, s32[2]{0:T(128)}, u32[]{:S(2)}) copy-start(s32[2]{0:T(128)} %rows.1) | copy-start | bytes 28
  122.5 15.1 %copy-start.2 = (f32[1,256,512]{2,1,0:T(8,128)S(1)}, f32[1,256,512]{2,1,0:T(8,128)}, u32[]{:S(2)}) copy-start(f32[1,256,512]{2,1,0:T(8,128)} %param.5) | copy-start | bytes 1572868
  137.6 1.0 copy-start.4
Sparse Core Ops, SparseCore 0:
  42.6 63.9 all-gather.2

commit v6 on v3

--- a/solution.py
+++ b/solution.py
@@ -5,7 +5,7 @@
 from jax.experimental.pallas import tpu as pltpu
 from jax.sharding import Mesh, PartitionSpec as P
 
-PLANE = 8
+LINES, CORES = 4, 2
 PANEL = 32
 OUTER = (((0,), (0,)), ((), ()))
 ROWS = (((1,), (1,)), ((), ()))
@@ -28,11 +28,6 @@
         OUTER,
         preferred_element_type=jnp.float32,
     )
-
-
-def recip(d):
-    r = pl.reciprocal(d, approx=True)
-    return r * (2.0 - d * r)
 
 
 def lane_block(x, lo, count):
@@ -72,7 +67,7 @@
             at, s = k // 8, k % 8
             col = cols[k]
             d = jnp.broadcast_to(col[at][s : s + 1], (8, 128))
-            r = recip(d)
+            r = pl.reciprocal(d, approx=True)
             scale[at] = jnp.where(sub == s, lax.rsqrt(d), scale[at])
             if k == PANEL - 1:
                 break
@@ -135,34 +130,37 @@
     return pattern[part, row].astype(jnp.float32)
 
 
-def pivot_kernel(row_ref, pattern, blocks, own, lead, below, second, mine):
+def pivot_kernel(blocks, solver):
+    size, half = solver.shape[1:]
+    cores, lines = blocks.shape[:2]
+
+    def gather(k):
+        return jnp.concatenate([blocks[c, y, k] for y in range(lines) for c in range(cores)])
+
+    w00 = inverse_factor(gather(0))
+    solver[0] = w00
+    l10 = dot6(split(gather(1)), split(w00))
+    solver[1] = l10
+    l10 = split(l10)
+    solver[2] = inverse_factor(gather(2) - dot6(l10, l10))
+
+
+def update_kernel(row_ref, pattern, rows, targets, solver, own, trailing, mine, out):
     size, width = own.shape
     half = width // 2
     row = row_ref[0]
-    w00 = inverse_factor(blocks[:, 0].reshape(size, half))
-    lead[...] = w00
-    w00 = split(w00)
-    l10 = dot6(split(blocks[:, 1].reshape(size, half)), w00)
-    below[...] = l10
-    l10 = split(l10)
-    w11 = inverse_factor(blocks[:, 2].reshape(size, half) - dot6(l10, l10))
-    second[...] = w11
-    w11 = split(w11)
+    w00, l10, w11 = split(solver[0]), split(solver[1]), split(solver[2])
     one = dot6(split(own[:, :half] * flag(pattern, 0, row)), w00)
     inner = own[:, half:] * flag(pattern, 1, row) - dot6(split(one), l10)
     two = dot6(split(inner), w11)
     shape = (size, half)
     upper = lax.broadcasted_iota(jnp.int32, shape, 0) < lax.broadcasted_iota(jnp.int32, shape, 1)
-    mine[:, :half] = jnp.where(upper & (row == 0), 0.0, one)
-    mine[:, half:] = jnp.where((upper & (row == 1)) | (row == 0), 0.0, two)
-
-
-def update_kernel(row_ref, pattern, rows, targets, lead, below, second, mine, trailing, out):
-    size, width = mine.shape
-    half = width // 2
-    w00, l10, w11 = split(lead[...]), split(below[...]), split(second[...])
-    left, right = split(mine[:, :half]), split(mine[:, half:])
-    keep = (row_ref[0] >= 2).astype(jnp.float32)
+    one = jnp.where(upper & (row == 0), 0.0, one)
+    two = jnp.where((upper & (row == 1)) | (row == 0), 0.0, two)
+    mine[:, :half] = one
+    mine[:, half:] = two
+    left, right = split(one), split(two)
+    keep = (row >= 2).astype(jnp.float32)
     for t in range(targets.shape[1]):
         block = targets[:, t].reshape(size, width)
         one = split(dot3(split(block[:, :half] * flag(pattern, 0, rows[t])), w00))
@@ -176,13 +174,12 @@
 def call(kernel, scalars, arrays, shapes, flops):
     specs = [pl.BlockSpec(memory_space=pltpu.SMEM)] * len(scalars)
     specs += [pl.BlockSpec(memory_space=pltpu.VMEM)] * len(arrays)
-    outs = [jax.ShapeDtypeStruct(shape, jnp.float32) for shape in shapes]
     return pl.pallas_call(
         kernel,
         in_specs=specs,
-        out_specs=[pl.BlockSpec(memory_space=pltpu.VMEM)] * len(outs),
-        out_shape=outs,
-        compiler_params=pltpu.CompilerParams(vmem_limit_bytes=32 << 20),
+        out_specs=[pl.BlockSpec(memory_space=pltpu.VMEM)] * len(shapes),
+        out_shape=[jax.ShapeDtypeStruct(shape, jnp.float32) for shape in shapes],
+        compiler_params=pltpu.CompilerParams(vmem_limit_bytes=16 << 20),
         cost_estimate=pl.CostEstimate(flops=flops, bytes_accessed=1 << 20, transcendentals=0),
     )(*scalars, *arrays)
 
@@ -198,13 +195,14 @@
 def local(panel, trailing, pattern, target_rows):
     _, size, width = panel.shape
     half = width // 2
-    nz, npl = lax.axis_size("z"), lax.axis_size("p")
-    row = (lax.axis_index("z") * npl + lax.axis_index("p")).astype(jnp.int32)[None]
+    plane = ("y", "core")
+    nz, npl = lax.axis_size("z"), lax.axis_size(plane)
+    row = (lax.axis_index("z") * npl + lax.axis_index(plane)).astype(jnp.int32)[None]
     count = target_rows.shape[0]
     own = panel[0]
     coarse, lanes = size // npl, width // 128
     sub = coarse * lanes // nz
-    pieces = lax.all_to_all(own.reshape(npl, coarse, width), "p", 0, 0)
+    pieces = lax.all_to_all(own.reshape(npl, coarse, width), plane, 0, 0)
     chosen = [pieces[0], pieces[1]]
     chosen += [pick(pieces, target_rows[t] % npl, 0) for t in range(count)]
     wanted = len(chosen)
@@ -217,21 +215,15 @@
     held = held.reshape(coarse // sub, lanes, wanted, sub, 128).transpose(2, 0, 3, 1, 4)
     held = held.reshape(wanted, coarse, width)
     blocks = jnp.stack([held[0, :, :half], held[1, :, :half], held[1, :, half:]])
-    blocks = lax.all_to_all(copies(blocks, npl), "p", 0, 0)
-    targets = lax.all_to_all(copies(held[2:], npl), "p", 0, 0)
-    square = (size, half)
-    lead, below, second, mine = call(
-        pivot_kernel,
-        (row, pattern),
-        (blocks, own),
-        (square, square, square, (size, width)),
-        1 << 34,
-    )
-    (schur,) = call(
+    blocks = lax.all_to_all(copies(blocks, lax.axis_size("y")), "y", 0, 0)
+    blocks = lax.all_gather(blocks, "core", axis=0)
+    targets = lax.all_to_all(copies(held[2:], npl), plane, 0, 0)
+    (solver,) = call(pivot_kernel, (), (blocks,), ((3, size, half),), 1 << 34)
+    mine, schur = call(
         update_kernel,
         (row, pattern, target_rows),
-        (targets, lead, below, second, mine, trailing[0]),
-        ((size, trailing.shape[2]),),
+        (targets, solver, own, trailing[0]),
+        ((size, width), (size, trailing.shape[2])),
         1 << 30,
     )
     return mine[None], schur[None]
@@ -239,8 +231,9 @@
 
 def solution(mesh):
     blk, col = mesh.devices.shape
-    inner = Mesh(mesh.devices.reshape(blk // PLANE, PLANE, col), ("z", "p", "x"))
-    rows = ("z", "p")
+    inner = mesh.devices.reshape(blk // (LINES * CORES), LINES, CORES, col)
+    inner = Mesh(inner, ("z", "y", "core", "x"))
+    rows = ("z", "y", "core")
     in_specs = (P(None, rows, None), P(None, rows, "x"), P(), P("x"))
     out_specs = (P(None, rows, None), P(None, rows, "x"))
     return jax.shard_map(local, mesh=inner, in_specs=in_specs, out_specs=out_specs, check_vma=False)

time: 121 us -> 113 us (0.934)
  waiting for transfers between devices: 29.3 us -> 23.2 us
  local copies, waits for them, and re-layouts: 6.89 us -> 3.95 us
  blocking collectives: 24 us -> 26.3 us
  Pallas kernels: 19.6 us -> 17.7 us
    all_to_all x3, waiting for transfers between devices: 17.6 us -> 11.5 us  [the longest x1 6.17 us: local(): blocks = lax.all_to_all(copies(blocks, lax.axis_size('y')), 'y', 0, 0)]
    unnamed x14 -> x8, local copies, waits for them, and re-layouts: 3.38 us -> 0.67 us
    all_gather x0 -> x1, blocking collectives: none -> 2.36 us  [local(): blocks = lax.all_gather(blocks, 'core', axis=0)]
    pallas_call x2, Pallas kernels: 19.6 us -> 17.7 us  [call(): pl.pallas_call(kernel, in_specs=specs, out_specs=[pl.BlockSpec(memory_spa...]
  transfers between devices with their start and end apart: 4 -> 4, of which waited for: 3 -> 3; matrix products, arithmetic and copies ran while one was open for 0% -> 1% of each run, Pallas kernels for 13% -> 12%
where the time goes in v6:
time: 113 us; the launch traced here: 112 us
  starting transfers between devices  35.3 us (31%)
  blocking collectives  26.3 us (23%)
  waiting for transfers between devices  23.2 us (21%)
  Pallas kernels  17.7 us (16%)
  between operations  5.66 us (5%)
  local copies, waits for them, and re-layouts  3.95 us (3%)
    all_to_all x1, blocking collectives, local(): held = lax.all_to_all(copies(jnp.concatenate(held), nz), 'z', 0, 0)  24 us
    pallas_call x2, Pallas kernels, call(): pl.pallas_call(kernel, in_specs=specs, out_specs=[pl.BlockSpec(memory_spa...  17.7 us
    all_to_all x1, waiting for transfers between devices, local(): got = lax.all_to_all(chosen, 'z', 0, 0).reshape(nz, wanted, sub, 128)  11.7 us
    all_to_all x1, starting transfers between devices, local(): targets = lax.all_to_all(copies(held[2:], npl), plane, 0, 0)  11 us
    all_to_all x1, starting transfers between devices, local(): got = lax.all_to_all(chosen, 'z', 0, 0).reshape(nz, wanted, sub, 128)  10.6 us
    all_to_all x1, starting transfers between devices, local(): pieces = lax.all_to_all(own.reshape(npl, coarse, width), plane, 0, 0)  10.3 us
    all_to_all x1, waiting for transfers between devices, local(): blocks = lax.all_to_all(copies(blocks, lax.axis_size('y')), 'y', 0, 0)  6.17 us
    all_to_all x1, waiting for transfers between devices, local(): pieces = lax.all_to_all(own.reshape(npl, coarse, width), plane, 0, 0)  5.33 us
  transfers between devices with their start and end apart: 4, of which 3 were waited for; matrix products, arithmetic and copies ran while one was open for 1% of the time, Pallas kernels for 12%

profile of v6, /device:TPU:1, one launch (start us, length us, event | category | flops | bytes accessed | tf_op | source)
XLA Modules:
  0.0 112.2 jit_solution(14241625837570015603)
XLA Ops:
  0.6 0.0 copy-start.1
  0.6 10.3 %all-to-all-start = ((f32[8,32,512]{2,1,0:T(8,128)}), f32[8,32,512]{2,1,0:T(8,128)S(1)}, u32[]{:S(2)}, u32[]{:S(2)}) async-start(f32[8,32,512]{2,1,0:T(8,128)} %bitcast.32), calls=%async_computation | async-start | bytes 1048576 | tf_op jit(solution)/shard_map/all_to_all | solution.py:205
  10.9 0.0 copy-done.1
  10.9 0.6 fusion.1
  15.1 5.3 %all-to-all-done = f32[8,32,512]{2,1,0:T(8,128)S(1)} async-done(((f32[8,32,512]{2,1,0:T(8,128)}), f32[8,32,512]{2,1,0:T(8,128)S(1)}, u32[]{:S(2)}, u32[]{:S(2)}) %all-to-all-start) | async-done | bytes 524320 | tf_op jit(solution)/shard_map/all_to_all | solution.py:205
  20.5 0.7 copy.9
  21.2 10.6 %all-to-all-start.1 = ((f32[16,32,128]{2,1,0:T(8,128)}), f32[16,32,128]{2,1,0:T(8,128)S(1)}, u32[]{:S(2)}, u32[]{:S(2)}) async-start(f32[16,32,128]{2,1,0:T(8,128)} %bitcast.6), calls=%async_computation.1 | async-start | bytes 524288 | tf_op jit(solution)/shard_map/all_to_all | solution.py:211
  33.1 11.7 %all-to-all-done.1 = f32[16,32,128]{2,1,0:T(8,128)S(1)} async-done(((f32[16,32,128]{2,1,0:T(8,128)}), f32[16,32,128]{2,1,0:T(8,128)S(1)}, u32[]{:S(2)}, u32[]{:S(2)}) %all-to-all-start.1) | async-done | bytes 262176 | tf_op jit(solution)/shard_map/all_to_all | solution.py:211
  44.9 24.0 %all_to_all.25 = f32[16,32,128]{2,1,0:T(8,128)S(1)} all-to-all(f32[16,32,128]{2,1,0:T(8,128)S(1)} %broadcast_in_dim.30), channel_id=1, replica_groups=mesh['z'=16,'y'=4,'core'=2,'x'=4] {'z'}, dimensions={0} | all-to-all | bytes 524288 | tf_op jit(solution)/shard_map/all_to_all | solution.py:214
  68.9 0.8 broadcast_in_dim.33
  69.7 3.5 %all-to-all-start.4 = ((f32[4,3,32,256]{3,2,1,0:T(8,128)}), f32[4,3,32,256]{3,2,1,0:T(8,128)S(1)}, u32[]{:S(2)}, u32[]{:S(2)}) async-start(f32[4,3,32,256]{3,2,1,0:T(8,128)} %broadcast_in_dim.33), calls=%async_computation.4 | async-start | bytes 786432 | tf_op jit(solution)/shard_map/all_to_all | solution.py:218
  73.2 6.2 %all-to-all-done.4 = f32[4,3,32,256]{3,2,1,0:T(8,128)S(1)} async-done(((f32[4,3,32,256]{3,2,1,0:T(8,128)}), f32[4,3,32,256]{3,2,1,0:T(8,128)S(1)}, u32[]{:S(2)}, u32[]{:S(2)}) %all-to-all-start.4) | async-done | bytes 393248 | tf_op jit(solution)/shard_map/all_to_all | solution.py:218
  79.4 1.1 broadcast_in_dim.32
  80.5 11.0 %all-to-all-start.3 = ((f32[8,2,32,512]{3,2,1,0:T(8,128)}), f32[8,2,32,512]{3,2,1,0:T(8,128)S(1)}, u32[]{:S(2)}, u32[]{:S(2)}) async-start(f32[8,2,32,512]{3,2,1,0:T(8,128)} %broadcast_in_dim.32), calls=%async_computation.3 | async-start | bytes 2097152 | tf_op jit(solution)/shard_map/all_to_all | solution.py:220
  91.4 2.4 %all-gather = f32[8,3,32,256]{3,2,1,0:T(8,128)S(1)} all-gather(f32[4,3,32,256]{3,2,1,0:T(8,128)S(1)} %all-to-all-done.4), channel_id=2, replica_groups=mesh['z'=16,'y'=4,'core'=2,'x'=4] {'core'}, dimensions={0}, use_global_device_ids=true | all-gather | bytes 1179648 | tf_op jit(solution)/shard_map/all_gather | solution.py:219
  93.8 0.0 copy-start
  93.8 0.0 copy-start.2
  93.8 13.5 %shard_map.59.solver = f32[3,256,256]{2,1,0:T(8,128)S(1)} custom-call(f32[2,4,3,32,256]{4,3,2,1,0:T(8,128)S(1)} %bitcast.31), custom_call_target="tpu_custom_call" | custom-call | flops 17179869184 | bytes 1048576 | tf_op jit(solution)/shard_map/pallas_call | solution.py:177
  107.3 0.0 all-to-all-done.3.targets
  107.3 0.0 copy-start.3
  107.3 0.0 copy-done
  107.4 0.0 copy-done.2
  107.4 0.7 copy-done.3
  108.0 4.2 %shard_map.60 = (f32[256,512]{1,0:T(8,128)}, f32[256,512]{1,0:T(8,128)}) custom-call(s32[1]{0:T(128)} %bitcast.row_ref, s32[2,128]{1,0:T(2,128)S(1)} %copy-done.3, s32[2]{0:T(128)S(1)} %copy-done.1, f32[8,2,32,512]{3,2,1,0:T(8,128)S(1)} %all-to-all-done.3.targets, f32[3,256,256]{2,1,0:T(8,128)S(1)} %shard_map.59.solver, f32[256,512]{1,0:T(8,128)S(1)} %bitcast.33, ...), custom_call_target="tpu_custom_call" | custom-call | flops 1073741824 | bytes 1048576 | tf_op jit(solution)/shard_map/pallas_call | solution.py:177
  (13 shorter events, 0.1 us)
Async XLA Ops:
  0.6 10.3 %copy-start.1 = (s32[2]{0:T(128)S(1)}, s32[2]{0:T(128)}, u32[]{:S(2)}) copy-start(s32[2]{0:T(128)} %rows.1) | copy-start | bytes 28
  0.6 19.8 %all-to-all-start = ((f32[8,32,512]{2,1,0:T(8,128)}), f32[8,32,512]{2,1,0:T(8,128)S(1)}, u32[]{:S(2)}, u32[]{:S(2)}) async-start(f32[8,32,512]{2,1,0:T(8,128)} %bitcast.32), calls=%async_computation | async-start | bytes 1048576 | tf_op jit(solution)/shard_map/all_to_all | solution.py:205
  21.2 23.6 %all-to-all-start.1 = ((f32[16,32,128]{2,1,0:T(8,128)}), f32[16,32,128]{2,1,0:T(8,128)S(1)}, u32[]{:S(2)}, u32[]{:S(2)}) async-start(f32[16,32,128]{2,1,0:T(8,128)} %bitcast.6), calls=%async_computation.1 | async-start | bytes 524288 | tf_op jit(solution)/shard_map/all_to_all | solution.py:211
  69.7 9.7 %all-to-all-start.4 = ((f32[4,3,32,256]{3,2,1,0:T(8,128)}), f32[4,3,32,256]{3,2,1,0:T(8,128)S(1)}, u32[]{:S(2)}, u32[]{:S(2)}) async-start(f32[4,3,32,256]{3,2,1,0:T(8,128)} %broadcast_in_dim.33), calls=%async_computation.4 | async-start | bytes 786432 | tf_op jit(solution)/shard_map/all_to_all | solution.py:218
  80.5 26.8 %all-to-all-start.3 = ((f32[8,2,32,512]{3,2,1,0:T(8,128)}), f32[8,2,32,512]{3,2,1,0:T(8,128)S(1)}, u32[]{:S(2)}, u32[]{:S(2)}) async-start(f32[8,2,32,512]{3,2,1,0:T(8,128)} %broadcast_in_dim.32), calls=%async_computation.3 | async-start | bytes 2097152 | tf_op jit(solution)/shard_map/all_to_all | solution.py:220
  93.8 13.5 %copy-start = (f32[1,256,512]{2,1,0:T(8,128)S(1)}, f32[1,256,512]{2,1,0:T(8,128)}, u32[]{:S(2)}) copy-start(f32[1,256,512]{2,1,0:T(8,128)} %param.4) | copy-start | bytes 1572868
  93.8 13.6 %copy-start.2 = (f32[1,256,512]{2,1,0:T(8,128)S(1)}, f32[1,256,512]{2,1,0:T(8,128)}, u32[]{:S(2)}) copy-start(f32[1,256,512]{2,1,0:T(8,128)} %param.5) | copy-start | bytes 1572868
  107.3 0.7 copy-start.3

commit v7 on v6

--- a/solution.py
+++ b/solution.py
@@ -132,10 +132,16 @@
 
 def pivot_kernel(blocks, solver):
     size, half = solver.shape[1:]
-    cores, lines = blocks.shape[:2]
+    cores, lines, planes = blocks.shape[:3]
 
     def gather(k):
-        return jnp.concatenate([blocks[c, y, k] for y in range(lines) for c in range(cores)])
+        rows = [
+            [blocks[c, y, x, 2 * k + i] for i in range(2)]
+            for y in range(lines)
+            for c in range(cores)
+            for x in range(planes)
+        ]
+        return jnp.concatenate([jnp.concatenate(tiles, axis=1) for tiles in rows])
 
     w00 = inverse_factor(gather(0))
     solver[0] = w00
@@ -200,24 +206,32 @@
     row = (lax.axis_index("z") * npl + lax.axis_index(plane)).astype(jnp.int32)[None]
     count = target_rows.shape[0]
     own = panel[0]
-    coarse, lanes = size // npl, width // 128
-    sub = coarse * lanes // nz
+    nx = lax.axis_size("x")
+    coarse, fine, lanes = size // npl, size // (npl * nx), width // 128
+    assert coarse * lanes == 8 * nz and fine == 8 and lanes * 4 == nz
     pieces = lax.all_to_all(own.reshape(npl, coarse, width), plane, 0, 0)
-    chosen = [pieces[0], pieces[1]]
-    chosen += [pick(pieces, target_rows[t] % npl, 0) for t in range(count)]
-    wanted = len(chosen)
-    chosen = jnp.stack(chosen).reshape(wanted, coarse // sub, sub, lanes, 128)
-    chosen = chosen.transpose(1, 3, 0, 2, 4).reshape(nz, wanted * sub, 128)
-    got = lax.all_to_all(chosen, "z", 0, 0).reshape(nz, wanted, sub, 128)
-    held = [got[0, 0], got[0, 1]]
-    held += [pick(got[:, 2 + t], target_rows[t] // npl, 0) for t in range(count)]
-    held = lax.all_to_all(copies(jnp.concatenate(held), nz), "z", 0, 0)
-    held = held.reshape(coarse // sub, lanes, wanted, sub, 128).transpose(2, 0, 3, 1, 4)
-    held = held.reshape(wanted, coarse, width)
-    blocks = jnp.stack([held[0, :, :half], held[1, :, :half], held[1, :, half:]])
-    blocks = lax.all_to_all(copies(blocks, lax.axis_size("y")), "y", 0, 0)
+    chosen = jnp.stack([pick(pieces, target_rows[t] % npl, 0) for t in range(count)])
+    chosen = chosen.reshape(count, coarse // 8, 8, lanes, 128).transpose(1, 3, 0, 2, 4)
+    share = lax.dynamic_slice_in_dim(pieces[:2], lax.axis_index("x") * fine, fine, 1)
+    share = share.reshape(2, 2, 4, lanes, 128).transpose(0, 3, 1, 2, 4)
+    part = jnp.concatenate(
+        [chosen.reshape(nz, 2 * count, 4, 128), share.reshape(nz, 1, 4, 128)], axis=1
+    )
+    got = lax.all_to_all(part, "z", 0, 0)
+    part = [
+        lax.dynamic_slice(got, (target_rows[t] // npl, 2 * t, 0, 0), (1, 2, 4, 128))[0]
+        for t in range(count)
+    ]
+    part = jnp.concatenate(part + [got[0, 2 * count :]])
+    part = lax.all_to_all(copies(part, nz), "z", 0, 0)
+    held = part[:, : 2 * count].reshape(coarse // 8, lanes, count, 8, 128)
+    held = held.transpose(2, 0, 3, 1, 4).reshape(count, coarse, width)
+    share = part[:, 2 * count].reshape(2, lanes, 8, 128)
+    share = jnp.concatenate([share[0, : lanes // 2], share[1]])
+    blocks = lax.all_to_all(copies(share, LINES * nx), ("y", "x"), 0, 0)
     blocks = lax.all_gather(blocks, "core", axis=0)
-    targets = lax.all_to_all(copies(held[2:], npl), plane, 0, 0)
+    blocks = blocks.reshape((CORES, LINES, nx) + share.shape)
+    targets = lax.all_to_all(copies(held, npl), plane, 0, 0)
     (solver,) = call(pivot_kernel, (), (blocks,), ((3, size, half),), 1 << 34)
     mine, schur = call(
         update_kernel,

time: 113 us -> 109 us (0.965)
  blocking collectives: 26.3 us -> 21.9 us
    all_to_all x1, blocking collectives: 24 us -> 19.5 us  [local(): part = lax.all_to_all(copies(part, nz), 'z', 0, 0)]
    all_to_all x3, waiting for transfers between devices: 17.9 us -> 19.1 us  [the longest x1 10.9 us: local(): got = lax.all_to_all(part, 'z', 0, 0)]
where the time goes in v7:
time: 109 us
  starting transfers between devices  34.9 us (32%)
  waiting for transfers between devices  23.4 us (21%)
  blocking collectives  21.9 us (20%)
  Pallas kernels  17.7 us (16%)
  between operations  5.96 us (5%)
  local copies, waits for them, and re-layouts  4 us (4%)
    all_to_all x1, blocking collectives, local(): part = lax.all_to_all(copies(part, nz), 'z', 0, 0)  19.5 us
    pallas_call x2, Pallas kernels, call(): pl.pallas_call(kernel, in_specs=specs, out_specs=[pl.BlockSpec(memory_spa...  17.7 us
    all_to_all x1, waiting for transfers between devices, local(): got = lax.all_to_all(part, 'z', 0, 0)  10.9 us
    all_to_all x1, starting transfers between devices, local(): got = lax.all_to_all(part, 'z', 0, 0)  10.6 us
    all_to_all x1, starting transfers between devices, local(): pieces = lax.all_to_all(own.reshape(npl, coarse, width), plane, 0, 0)  10.3 us
    all_to_all x1, starting transfers between devices, local(): targets = lax.all_to_all(copies(held, npl), plane, 0, 0)  9.27 us
    all_to_all x1, waiting for transfers between devices, local(): blocks = lax.all_to_all(copies(share, LINES * nx), ('y', 'x'), 0, 0)  8.2 us
    all_to_all x1, starting transfers between devices, local(): blocks = lax.all_to_all(copies(share, LINES * nx), ('y', 'x'), 0, 0)  4.73 us
  transfers between devices with their start and end apart: 4, of which 3 were waited for; matrix products, arithmetic and copies ran while one was open for 1% of the time, Pallas kernels for 12%

profile of v7, /device:TPU:1, one launch (start us, length us, event | category | flops | bytes accessed | tf_op | source)
XLA Modules:
  0.0 108.6 jit_solution(15402990862542680130)
XLA Ops:
  0.6 10.3 %all-to-all-start = ((f32[8,32,512]{2,1,0:T(8,128)}), f32[8,32,512]{2,1,0:T(8,128)S(1)}, u32[]{:S(2)}, u32[]{:S(2)}) async-start(f32[8,32,512]{2,1,0:T(8,128)} %bitcast.33), calls=%async_computation | async-start | bytes 1048576 | tf_op jit(solution)/shard_map/all_to_all | solution.py:212
  10.9 0.0 copy-start.1
  10.9 0.7 copy-done.1
  11.6 0.6 fusion
  16.1 4.4 %all-to-all-done = f32[8,32,512]{2,1,0:T(8,128)S(1)} async-done(((f32[8,32,512]{2,1,0:T(8,128)}), f32[8,32,512]{2,1,0:T(8,128)S(1)}, u32[]{:S(2)}, u32[]{:S(2)}) %all-to-all-start) | async-done | bytes 524320 | tf_op jit(solution)/shard_map/all_to_all | solution.py:212
  20.6 0.7 pad_maximum_fusion
  21.3 10.6 %all-to-all-start.1 = ((f32[16,5,4,128]{3,2,1,0:T(4,128)}), f32[16,5,4,128]{3,2,1,0:T(4,128)S(1)}, u32[]{:S(2)}, u32[]{:S(2)}) async-start(f32[16,5,4,128]{3,2,1,0:T(4,128)} %pad_maximum_fusion), calls=%async_computation.1 | async-start | bytes 327680 | tf_op jit(solution)/shard_map/all_to_all | solution.py:220
  33.2 10.9 %all-to-all-done.1 = f32[16,5,4,128]{3,2,1,0:T(4,128)S(1)} async-done(((f32[16,5,4,128]{3,2,1,0:T(4,128)}), f32[16,5,4,128]{3,2,1,0:T(4,128)S(1)}, u32[]{:S(2)}, u32[]{:S(2)}) %all-to-all-start.1) | async-done | bytes 163872 | tf_op jit(solution)/shard_map/all_to_all | solution.py:220
  44.1 19.5 %all_to_all.25 = f32[16,5,4,128]{3,2,1,0:T(4,128)S(1)} all-to-all(f32[16,5,4,128]{3,2,1,0:T(4,128)S(1)} %broadcast_in_dim.29), channel_id=1, replica_groups=mesh['z'=16,'y'=4,'core'=2,'x'=4] {'z'}, dimensions={0} | all-to-all | bytes 327680 | tf_op jit(solution)/shard_map/all_to_all | solution.py:226
  63.7 0.8 broadcast_in_dim.32
  64.5 4.7 %all-to-all-start.4 = ((f32[16,6,8,128]{3,2,1,0:T(8,128)}), f32[16,6,8,128]{3,2,1,0:T(8,128)S(1)}, u32[]{:S(2)}, u32[]{:S(2)}) async-start(f32[16,6,8,128]{3,2,1,0:T(8,128)} %broadcast_in_dim.32), calls=%async_computation.4 | async-start | bytes 786432 | tf_op jit(solution)/shard_map/all_to_all | solution.py:231
  69.3 8.2 %all-to-all-done.4 = f32[16,6,8,128]{3,2,1,0:T(8,128)S(1)} async-done(((f32[16,6,8,128]{3,2,1,0:T(8,128)}), f32[16,6,8,128]{3,2,1,0:T(8,128)S(1)}, u32[]{:S(2)}, u32[]{:S(2)}) %all-to-all-start.4) | async-done | bytes 393248 | tf_op jit(solution)/shard_map/all_to_all | solution.py:231
  77.5 1.1 %broadcast_in_dim.31 = f32[8,2,32,512]{3,2,1,0:T(8,128)} broadcast(f32[2,32,512]{2,1,0:T(8,128)S(1)} %bitcast.36), dimensions={1,2,3} | broadcast | bytes 1179648 | tf_op jit(solution)/shard_map/broadcast_in_dim | solution.py:194
  78.6 9.3 %all-to-all-start.3 = ((f32[8,2,32,512]{3,2,1,0:T(8,128)}), f32[8,2,32,512]{3,2,1,0:T(8,128)S(1)}, u32[]{:S(2)}, u32[]{:S(2)}) async-start(f32[8,2,32,512]{3,2,1,0:T(8,128)} %broadcast_in_dim.31), calls=%async_computation.3 | async-start | bytes 2097152 | tf_op jit(solution)/shard_map/all_to_all | solution.py:234
  87.8 2.4 %all-gather = f32[32,6,8,128]{3,2,1,0:T(8,128)S(1)} all-gather(f32[16,6,8,128]{3,2,1,0:T(8,128)S(1)} %all-to-all-done.4), channel_id=2, replica_groups=mesh['z'=16,'y'=4,'core'=2,'x'=4] {'core'}, dimensions={0}, use_global_device_ids=true | all-gather | bytes 1179648 | tf_op jit(solution)/shard_map/all_gather | solution.py:232
  90.2 0.0 copy-start
  90.2 0.0 copy-start.2
  90.2 13.5 %shard_map.59.solver = f32[3,256,256]{2,1,0:T(8,128)S(1)} custom-call(f32[2,4,4,6,8,128]{5,4,3,2,1,0:T(8,128)S(1)} %bitcast.32), custom_call_target="tpu_custom_call" | custom-call | flops 17179869184 | bytes 1048576 | tf_op jit(solution)/shard_map/pallas_call | solution.py:183
  103.7 0.0 all-to-all-done.3.targets
  103.7 0.0 copy-start.3
  103.7 0.0 copy-done
  103.7 0.0 copy-done.2
  103.8 0.7 copy-done.3
  104.4 4.2 %shard_map.60 = (f32[256,512]{1,0:T(8,128)}, f32[256,512]{1,0:T(8,128)}) custom-call(s32[1]{0:T(128)} %bitcast.row_ref, s32[2,128]{1,0:T(2,128)S(1)} %copy-done.3, s32[2]{0:T(128)S(1)} %copy-done.1, f32[8,2,32,512]{3,2,1,0:T(8,128)S(1)} %all-to-all-done.3.targets, f32[3,256,256]{2,1,0:T(8,128)S(1)} %shard_map.59.solver, f32[256,512]{1,0:T(8,128)S(1)} %bitcast.34, ...), custom_call_target="tpu_custom_call" | custom-call | flops 1073741824 | bytes 1048576 | tf_op jit(solution)/shard_map/pallas_call | solution.py:183
  (18 shorter events, 0.2 us)
Async XLA Ops:
  0.6 19.8 %all-to-all-start = ((f32[8,32,512]{2,1,0:T(8,128)}), f32[8,32,512]{2,1,0:T(8,128)S(1)}, u32[]{:S(2)}, u32[]{:S(2)}) async-start(f32[8,32,512]{2,1,0:T(8,128)} %bitcast.33), calls=%async_computation | async-start | bytes 1048576 | tf_op jit(solution)/shard_map/all_to_all | solution.py:212
  10.9 0.7 copy-start.1
  21.3 22.8 %all-to-all-start.1 = ((f32[16,5,4,128]{3,2,1,0:T(4,128)}), f32[16,5,4,128]{3,2,1,0:T(4,128)S(1)}, u32[]{:S(2)}, u32[]{:S(2)}) async-start(f32[16,5,4,128]{3,2,1,0:T(4,128)} %pad_maximum_fusion), calls=%async_computation.1 | async-start | bytes 327680 | tf_op jit(solution)/shard_map/all_to_all | solution.py:220
  64.5 13.0 %all-to-all-start.4 = ((f32[16,6,8,128]{3,2,1,0:T(8,128)}), f32[16,6,8,128]{3,2,1,0:T(8,128)S(1)}, u32[]{:S(2)}, u32[]{:S(2)}) async-start(f32[16,6,8,128]{3,2,1,0:T(8,128)} %broadcast_in_dim.32), calls=%async_computation.4 | async-start | bytes 786432 | tf_op jit(solution)/shard_map/all_to_all | solution.py:231
  78.6 25.1 %all-to-all-start.3 = ((f32[8,2,32,512]{3,2,1,0:T(8,128)}), f32[8,2,32,512]{3,2,1,0:T(8,128)S(1)}, u32[]{:S(2)}, u32[]{:S(2)}) async-start(f32[8,2,32,512]{3,2,1,0:T(8,128)} %broadcast_in_dim.31), calls=%async_computation.3 | async-start | bytes 2097152 | tf_op jit(solution)/shard_map/all_to_all | solution.py:234
  90.2 13.5 %copy-start = (f32[1,256,512]{2,1,0:T(8,128)S(1)}, f32[1,256,512]{2,1,0:T(8,128)}, u32[]{:S(2)}) copy-start(f32[1,256,512]{2,1,0:T(8,128)} %param.4) | copy-start | bytes 1572868
  90.2 13.5 %copy-start.2 = (f32[1,256,512]{2,1,0:T(8,128)S(1)}, f32[1,256,512]{2,1,0:T(8,128)}, u32[]{:S(2)}) copy-start(f32[1,256,512]{2,1,0:T(8,128)} %param.5) | copy-start | bytes 1572868
  103.7 0.7 copy-start.3

commit v8 on v7

--- a/solution.py
+++ b/solution.py
@@ -6,7 +6,7 @@
 from jax.sharding import Mesh, PartitionSpec as P
 
 LINES, CORES = 4, 2
-PANEL = 32
+PANEL, STEP = 32, 16
 OUTER = (((0,), (0,)), ((), ()))
 ROWS = (((1,), (1,)), ((), ()))
 
@@ -46,15 +46,6 @@
         lo = PANEL * j
         rows, rest = rest[:PANEL], rest[PANEL:]
         tile, off = lo // 128, lo % 128
-        cols = [
-            [
-                jnp.broadcast_to(rows[8 * g : 8 * g + 8, lo + k : lo + k + 1], (8, 128))
-                if g >= k // 8
-                else None
-                for g in range(groups)
-            ]
-            for k in range(PANEL)
-        ]
         u = [
             [rows[8 * g : 8 * g + 8, 128 * c : 128 * c + 128] for c in range(tiles)]
             for g in range(groups)
@@ -63,28 +54,48 @@
             eye = (lane - off == sub + 8 * g).astype(jnp.float32)
             u[g][tile] = jnp.where(lane_block(eye, off, PANEL), eye, u[g][tile])
         scale = [jnp.zeros((8, 128), jnp.float32)] * groups
-        for k in range(PANEL):
-            at, s = k // 8, k % 8
-            col = cols[k]
-            d = jnp.broadcast_to(col[at][s : s + 1], (8, 128))
-            r = pl.reciprocal(d, approx=True)
-            scale[at] = jnp.where(sub == s, lax.rsqrt(d), scale[at])
-            if k == PANEL - 1:
-                break
-            low = [None] * at + [jnp.where(sub > s, col[at], 0.0)] + col[at + 1 :]
-            ratio = [None if x is None else x * r for x in low]
-            for i in range(k + 1, PANEL):
-                first = i // 8
-                b = jnp.broadcast_to(col[first][i % 8 : i % 8 + 1], (8, 128))
-                for g in range(first, groups):
-                    if i == k + 1:
-                        cols[i][g] = cols[i][g] - (low[g] * b) * r
-                    else:
+        block = [rows[8 * g : 8 * g + 8, 128 * tile : 128 * tile + 128] for g in range(groups)]
+        for start in range(0, PANEL, STEP):
+            stop = start + STEP
+            cols = {
+                k: {
+                    g: jnp.broadcast_to(block[g][:, off + k : off + k + 1], (8, 128))
+                    for g in range(k // 8, groups)
+                }
+                for k in range(start, stop)
+            }
+
+            def spread(i, k, cols=cols):
+                return jnp.broadcast_to(cols[k][i // 8][i % 8 : i % 8 + 1], (8, 128))
+
+            d = spread(start, start)
+            b1 = spread(start + 1, start)
+            for k in range(start, stop):
+                at, s = k // 8, k % 8
+                col = cols[k]
+                r = pl.reciprocal(d, approx=True)
+                scale[at] = jnp.where(sub == s, lax.rsqrt(d), scale[at])
+                low = {g: jnp.where(sub > s, x, 0.0) if g == at else x for g, x in col.items()}
+                ratio = {g: x * r for g, x in low.items()}
+                if k + 1 < stop:
+                    b = b1
+                    d = spread(k + 1, k + 1) - (b * b) * r
+                    if k + 2 < stop:
+                        b1 = spread(k + 2, k + 1) - (spread(k + 2, k) * b) * r
+                    for g in cols[k + 1]:
+                        cols[k + 1][g] = cols[k + 1][g] - (low[g] * b) * r
+                for i in range(k + 2, stop):
+                    b = spread(i, k)
+                    for g in cols[i]:
                         cols[i][g] = cols[i][g] - ratio[g] * b
-            for c in range(tiles):
-                b = jnp.broadcast_to(u[at][c][s : s + 1], (8, 128))
-                for g in range(at if s < 7 else at + 1, groups):
-                    u[g][c] = u[g][c] - ratio[g] * b
+                if stop < PANEL:
+                    b = jnp.broadcast_to(block[at][s : s + 1], (8, 128))
+                    for g in range(at if s < 7 else at + 1, groups):
+                        block[g] = block[g] - ratio[g] * b
+                for c in range(tiles):
+                    b = jnp.broadcast_to(u[at][c][s : s + 1], (8, 128))
+                    for g in range(at if s < 7 else at + 1, groups):
+                        u[g][c] = u[g][c] - ratio[g] * b
         u = jnp.concatenate(
             [
                 jnp.concatenate([x * scale[g] for x in u[g]], axis=1)

time: 109 us -> 108 us (level)
  transfers between devices with their start and end apart: 4 -> 4, of which waited for: 3 -> 4; matrix products, arithmetic and copies ran while one was open for 1% -> 1% of each run, Pallas kernels for 12% -> 12%
where the time goes in v8:
time: 108 us
  starting transfers between devices  34.9 us (32%)
  waiting for transfers between devices  23.5 us (22%)
  blocking collectives  21.9 us (20%)
  Pallas kernels  16.9 us (16%)
  between operations  5.93 us (5%)
  local copies, waits for them, and re-layouts  4.02 us (4%)
    all_to_all x1, blocking collectives, local(): part = lax.all_to_all(copies(part, nz), 'z', 0, 0)  19.5 us
    pallas_call x2, Pallas kernels, call(): pl.pallas_call(kernel, in_specs=specs, out_specs=[pl.BlockSpec(memory_spa...  16.9 us
    all_to_all x1, waiting for transfers between devices, local(): got = lax.all_to_all(part, 'z', 0, 0)  10.9 us
    all_to_all x1, starting transfers between devices, local(): got = lax.all_to_all(part, 'z', 0, 0)  10.6 us
    all_to_all x1, starting transfers between devices, local(): pieces = lax.all_to_all(own.reshape(npl, coarse, width), plane, 0, 0)  10.3 us
    all_to_all x1, starting transfers between devices, local(): targets = lax.all_to_all(copies(held, npl), plane, 0, 0)  9.27 us
    all_to_all x1, waiting for transfers between devices, local(): blocks = lax.all_to_all(copies(share, LINES * nx), ('y', 'x'), 0, 0)  8.2 us
    all_to_all x1, starting transfers between devices, local(): blocks = lax.all_to_all(copies(share, LINES * nx), ('y', 'x'), 0, 0)  4.73 us
  transfers between devices with their start and end apart: 4, of which 4 were waited for; matrix products, arithmetic and copies ran while one was open for 1% of the time, Pallas kernels for 12%

profile of v8, /device:TPU:1, one launch (start us, length us, event | category | flops | bytes accessed | tf_op | source)
XLA Modules:
  0.0 107.9 jit_solution(6394463355504642372)
XLA Ops:
  0.6 10.3 %all-to-all-start = ((f32[8,32,512]{2,1,0:T(8,128)}), f32[8,32,512]{2,1,0:T(8,128)S(1)}, u32[]{:S(2)}, u32[]{:S(2)}) async-start(f32[8,32,512]{2,1,0:T(8,128)} %bitcast.33), calls=%async_computation | async-start | bytes 1048576 | tf_op jit(solution)/shard_map/all_to_all | solution.py:223
  10.9 0.0 copy-start.1
  10.9 0.7 copy-done.1
  11.6 0.6 fusion
  16.1 4.4 %all-to-all-done = f32[8,32,512]{2,1,0:T(8,128)S(1)} async-done(((f32[8,32,512]{2,1,0:T(8,128)}), f32[8,32,512]{2,1,0:T(8,128)S(1)}, u32[]{:S(2)}, u32[]{:S(2)}) %all-to-all-start) | async-done | bytes 524320 | tf_op jit(solution)/shard_map/all_to_all | solution.py:223
  20.6 0.7 pad_maximum_fusion
  21.3 10.6 %all-to-all-start.1 = ((f32[16,5,4,128]{3,2,1,0:T(4,128)}), f32[16,5,4,128]{3,2,1,0:T(4,128)S(1)}, u32[]{:S(2)}, u32[]{:S(2)}) async-start(f32[16,5,4,128]{3,2,1,0:T(4,128)} %pad_maximum_fusion), calls=%async_computation.1 | async-start | bytes 327680 | tf_op jit(solution)/shard_map/all_to_all | solution.py:231
  33.2 10.9 %all-to-all-done.1 = f32[16,5,4,128]{3,2,1,0:T(4,128)S(1)} async-done(((f32[16,5,4,128]{3,2,1,0:T(4,128)}), f32[16,5,4,128]{3,2,1,0:T(4,128)S(1)}, u32[]{:S(2)}, u32[]{:S(2)}) %all-to-all-start.1) | async-done | bytes 163872 | tf_op jit(solution)/shard_map/all_to_all | solution.py:231
  44.1 19.5 %all_to_all.25 = f32[16,5,4,128]{3,2,1,0:T(4,128)S(1)} all-to-all(f32[16,5,4,128]{3,2,1,0:T(4,128)S(1)} %broadcast_in_dim.29), channel_id=1, replica_groups=mesh['z'=16,'y'=4,'core'=2,'x'=4] {'z'}, dimensions={0} | all-to-all | bytes 327680 | tf_op jit(solution)/shard_map/all_to_all | solution.py:237
  63.7 0.8 broadcast_in_dim.32
  64.5 4.7 %all-to-all-start.4 = ((f32[16,6,8,128]{3,2,1,0:T(8,128)}), f32[16,6,8,128]{3,2,1,0:T(8,128)S(1)}, u32[]{:S(2)}, u32[]{:S(2)}) async-start(f32[16,6,8,128]{3,2,1,0:T(8,128)} %broadcast_in_dim.32), calls=%async_computation.4 | async-start | bytes 786432 | tf_op jit(solution)/shard_map/all_to_all | solution.py:242
  69.3 8.2 %all-to-all-done.4 = f32[16,6,8,128]{3,2,1,0:T(8,128)S(1)} async-done(((f32[16,6,8,128]{3,2,1,0:T(8,128)}), f32[16,6,8,128]{3,2,1,0:T(8,128)S(1)}, u32[]{:S(2)}, u32[]{:S(2)}) %all-to-all-start.4) | async-done | bytes 393248 | tf_op jit(solution)/shard_map/all_to_all | solution.py:242
  77.5 1.1 %broadcast_in_dim.31 = f32[8,2,32,512]{3,2,1,0:T(8,128)} broadcast(f32[2,32,512]{2,1,0:T(8,128)S(1)} %bitcast.36), dimensions={1,2,3} | broadcast | bytes 1179648 | tf_op jit(solution)/shard_map/broadcast_in_dim | solution.py:205
  78.6 9.3 %all-to-all-start.3 = ((f32[8,2,32,512]{3,2,1,0:T(8,128)}), f32[8,2,32,512]{3,2,1,0:T(8,128)S(1)}, u32[]{:S(2)}, u32[]{:S(2)}) async-start(f32[8,2,32,512]{3,2,1,0:T(8,128)} %broadcast_in_dim.31), calls=%async_computation.3 | async-start | bytes 2097152 | tf_op jit(solution)/shard_map/all_to_all | solution.py:245
  87.8 2.4 %all-gather = f32[32,6,8,128]{3,2,1,0:T(8,128)S(1)} all-gather(f32[16,6,8,128]{3,2,1,0:T(8,128)S(1)} %all-to-all-done.4), channel_id=2, replica_groups=mesh['z'=16,'y'=4,'core'=2,'x'=4] {'core'}, dimensions={0}, use_global_device_ids=true | all-gather | bytes 1179648 | tf_op jit(solution)/shard_map/all_gather | solution.py:243
  90.2 0.0 copy-start
  90.2 0.0 copy-start.2
  90.2 12.6 %shard_map.59.solver = f32[3,256,256]{2,1,0:T(8,128)S(1)} custom-call(f32[2,4,4,6,8,128]{5,4,3,2,1,0:T(8,128)S(1)} %bitcast.32), custom_call_target="tpu_custom_call" | custom-call | flops 17179869184 | bytes 1048576 | tf_op jit(solution)/shard_map/pallas_call | solution.py:194
  102.8 0.1 all-to-all-done.3.targets
  103.0 0.0 copy-start.3
  103.0 0.0 copy-done
  103.0 0.0 copy-done.2
  103.0 0.7 copy-done.3
  103.6 4.2 %shard_map.60 = (f32[256,512]{1,0:T(8,128)}, f32[256,512]{1,0:T(8,128)}) custom-call(s32[1]{0:T(128)} %bitcast.row_ref, s32[2,128]{1,0:T(2,128)S(1)} %copy-done.3, s32[2]{0:T(128)S(1)} %copy-done.1, f32[8,2,32,512]{3,2,1,0:T(8,128)S(1)} %all-to-all-done.3.targets, f32[3,256,256]{2,1,0:T(8,128)S(1)} %shard_map.59.solver, f32[256,512]{1,0:T(8,128)S(1)} %bitcast.34, ...), custom_call_target="tpu_custom_call" | custom-call | flops 1073741824 | bytes 1048576 | tf_op jit(solution)/shard_map/pallas_call | solution.py:194
  (18 shorter events, 0.2 us)
Async XLA Ops:
  0.6 19.8 %all-to-all-start = ((f32[8,32,512]{2,1,0:T(8,128)}), f32[8,32,512]{2,1,0:T(8,128)S(1)}, u32[]{:S(2)}, u32[]{:S(2)}) async-start(f32[8,32,512]{2,1,0:T(8,128)} %bitcast.33), calls=%async_computation | async-start | bytes 1048576 | tf_op jit(solution)/shard_map/all_to_all | solution.py:223
  10.9 0.7 copy-start.1
  21.3 22.8 %all-to-all-start.1 = ((f32[16,5,4,128]{3,2,1,0:T(4,128)}), f32[16,5,4,128]{3,2,1,0:T(4,128)S(1)}, u32[]{:S(2)}, u32[]{:S(2)}) async-start(f32[16,5,4,128]{3,2,1,0:T(4,128)} %pad_maximum_fusion), calls=%async_computation.1 | async-start | bytes 327680 | tf_op jit(solution)/shard_map/all_to_all | solution.py:231
  64.5 13.0 %all-to-all-start.4 = ((f32[16,6,8,128]{3,2,1,0:T(8,128)}), f32[16,6,8,128]{3,2,1,0:T(8,128)S(1)}, u32[]{:S(2)}, u32[]{:S(2)}) async-start(f32[16,6,8,128]{3,2,1,0:T(8,128)} %broadcast_in_dim.32), calls=%async_computation.4 | async-start | bytes 786432 | tf_op jit(solution)/shard_map/all_to_all | solution.py:242
  78.6 24.4 %all-to-all-start.3 = ((f32[8,2,32,512]{3,2,1,0:T(8,128)}), f32[8,2,32,512]{3,2,1,0:T(8,128)S(1)}, u32[]{:S(2)}, u32[]{:S(2)}) async-start(f32[8,2,32,512]{3,2,1,0:T(8,128)} %broadcast_in_dim.31), calls=%async_computation.3 | async-start | bytes 2097152 | tf_op jit(solution)/shard_map/all_to_all | solution.py:245
  90.2 12.8 %copy-start = (f32[1,256,512]{2,1,0:T(8,128)S(1)}, f32[1,256,512]{2,1,0:T(8,128)}, u32[]{:S(2)}) copy-start(f32[1,256,512]{2,1,0:T(8,128)} %param.4) | copy-start | bytes 1572868
  90.2 12.8 %copy-start.2 = (f32[1,256,512]{2,1,0:T(8,128)S(1)}, f32[1,256,512]{2,1,0:T(8,128)}, u32[]{:S(2)}) copy-start(f32[1,256,512]{2,1,0:T(8,128)} %param.5) | copy-start | bytes 1572868
  103.0 0.7 copy-start.3

commit v9 on v8

--- a/solution.py
+++ b/solution.py
@@ -162,14 +162,20 @@
     solver[2] = inverse_factor(gather(2) - dot6(l10, l10))
 
 
-def update_kernel(row_ref, pattern, rows, targets, solver, own, trailing, mine, out):
+def update_kernel(
+    row_ref, rows, pattern_ref, targets, solver, own, trailing, mine, out, pattern, done
+):
     size, width = own.shape
     half = width // 2
     row = row_ref[0]
+    fetch = pltpu.make_async_copy(pattern_ref, pattern, done)
+    fetch.start()
     w00, l10, w11 = split(solver[0]), split(solver[1]), split(solver[2])
-    one = dot6(split(own[:, :half] * flag(pattern, 0, row)), w00)
-    inner = own[:, half:] * flag(pattern, 1, row) - dot6(split(one), l10)
-    two = dot6(split(inner), w11)
+    one = dot3(split(own[:, :half]), w00)
+    fetch.wait()
+    one = jnp.where(pattern[0, row] != 0, one, 0.0)
+    inner = own[:, half:] * flag(pattern, 1, row) - dot3(split(one), l10)
+    two = dot3(split(inner), w11)
     shape = (size, half)
     upper = lax.broadcasted_iota(jnp.int32, shape, 0) < lax.broadcasted_iota(jnp.int32, shape, 1)
     one = jnp.where(upper & (row == 0), 0.0, one)
@@ -188,17 +194,19 @@
         out[:, at] = trailing[:, at] - keep * update
 
 
-def call(kernel, scalars, arrays, shapes, flops):
+def call(kernel, scalars, arrays, shapes, flops, raw=(), scratch=()):
     specs = [pl.BlockSpec(memory_space=pltpu.SMEM)] * len(scalars)
+    specs += [pl.BlockSpec(memory_space=pl.ANY)] * len(raw)
     specs += [pl.BlockSpec(memory_space=pltpu.VMEM)] * len(arrays)
     return pl.pallas_call(
         kernel,
         in_specs=specs,
         out_specs=[pl.BlockSpec(memory_space=pltpu.VMEM)] * len(shapes),
         out_shape=[jax.ShapeDtypeStruct(shape, jnp.float32) for shape in shapes],
+        scratch_shapes=scratch,
         compiler_params=pltpu.CompilerParams(vmem_limit_bytes=16 << 20),
         cost_estimate=pl.CostEstimate(flops=flops, bytes_accessed=1 << 20, transcendentals=0),
-    )(*scalars, *arrays)
+    )(*scalars, *raw, *arrays)
 
 
 def copies(x, count):
@@ -246,10 +254,12 @@
     (solver,) = call(pivot_kernel, (), (blocks,), ((3, size, half),), 1 << 34)
     mine, schur = call(
         update_kernel,
-        (row, pattern, target_rows),
+        (row, target_rows),
         (targets, solver, own, trailing[0]),
         ((size, width), (size, trailing.shape[2])),
         1 << 30,
+        (pattern,),
+        (pltpu.SMEM(pattern.shape, jnp.int32), pltpu.SemaphoreType.DMA),
     )
     return mine[None], schur[None]
 

time: 108 us -> 108 us (level)
  no operation moved by 1% of the time
where the time goes in v9:
time: 108 us
  starting transfers between devices  34.9 us (32%)
  waiting for transfers between devices  23.5 us (22%)
  blocking collectives  21.9 us (20%)
  Pallas kernels  16.8 us (16%)
  between operations  5.93 us (5%)
  local copies, waits for them, and re-layouts  4.02 us (4%)
    all_to_all x1, blocking collectives, local(): part = lax.all_to_all(copies(part, nz), 'z', 0, 0)  19.5 us
    pallas_call x2, Pallas kernels, call(): pl.pallas_call(kernel, in_specs=specs, out_specs=[pl.BlockSpec(memory_spa...  16.8 us
    all_to_all x1, waiting for transfers between devices, local(): got = lax.all_to_all(part, 'z', 0, 0)  10.9 us
    all_to_all x1, starting transfers between devices, local(): got = lax.all_to_all(part, 'z', 0, 0)  10.6 us
    all_to_all x1, starting transfers between devices, local(): pieces = lax.all_to_all(own.reshape(npl, coarse, width), plane, 0, 0)  10.3 us
    all_to_all x1, starting transfers between devices, local(): targets = lax.all_to_all(copies(held, npl), plane, 0, 0)  9.27 us
    all_to_all x1, waiting for transfers between devices, local(): blocks = lax.all_to_all(copies(share, LINES * nx), ('y', 'x'), 0, 0)  8.2 us
    all_to_all x1, starting transfers between devices, local(): blocks = lax.all_to_all(copies(share, LINES * nx), ('y', 'x'), 0, 0)  4.73 us
  transfers between devices with their start and end apart: 4, of which 4 were waited for; matrix products, arithmetic and copies ran while one was open for 1% of the time, Pallas kernels for 12%

profile of v9, /device:TPU:1, one launch (start us, length us, event | category | flops | bytes accessed | tf_op | source)
XLA Modules:
  0.0 107.8 jit_solution(14245554396281482020)
XLA Ops:
  0.6 10.3 %all-to-all-start = ((f32[8,32,512]{2,1,0:T(8,128)}), f32[8,32,512]{2,1,0:T(8,128)S(1)}, u32[]{:S(2)}, u32[]{:S(2)}) async-start(f32[8,32,512]{2,1,0:T(8,128)} %bitcast.33), calls=%async_computation | async-start | bytes 1048576 | tf_op jit(solution)/shard_map/all_to_all | solution.py:231
  10.9 0.0 copy-start.1
  10.9 0.7 copy-done.1
  11.6 0.6 fusion
  16.1 4.4 %all-to-all-done = f32[8,32,512]{2,1,0:T(8,128)S(1)} async-done(((f32[8,32,512]{2,1,0:T(8,128)}), f32[8,32,512]{2,1,0:T(8,128)S(1)}, u32[]{:S(2)}, u32[]{:S(2)}) %all-to-all-start) | async-done | bytes 524320 | tf_op jit(solution)/shard_map/all_to_all | solution.py:231
  20.6 0.7 pad_maximum_fusion
  21.3 10.6 %all-to-all-start.1 = ((f32[16,5,4,128]{3,2,1,0:T(4,128)}), f32[16,5,4,128]{3,2,1,0:T(4,128)S(1)}, u32[]{:S(2)}, u32[]{:S(2)}) async-start(f32[16,5,4,128]{3,2,1,0:T(4,128)} %pad_maximum_fusion), calls=%async_computation.1 | async-start | bytes 327680 | tf_op jit(solution)/shard_map/all_to_all | solution.py:239
  33.2 10.9 %all-to-all-done.1 = f32[16,5,4,128]{3,2,1,0:T(4,128)S(1)} async-done(((f32[16,5,4,128]{3,2,1,0:T(4,128)}), f32[16,5,4,128]{3,2,1,0:T(4,128)S(1)}, u32[]{:S(2)}, u32[]{:S(2)}) %all-to-all-start.1) | async-done | bytes 163872 | tf_op jit(solution)/shard_map/all_to_all | solution.py:239
  44.1 19.5 %all_to_all.25 = f32[16,5,4,128]{3,2,1,0:T(4,128)S(1)} all-to-all(f32[16,5,4,128]{3,2,1,0:T(4,128)S(1)} %broadcast_in_dim.29), channel_id=1, replica_groups=mesh['z'=16,'y'=4,'core'=2,'x'=4] {'z'}, dimensions={0} | all-to-all | bytes 327680 | tf_op jit(solution)/shard_map/all_to_all | solution.py:245
  63.7 0.8 broadcast_in_dim.32
  64.5 4.7 %all-to-all-start.4 = ((f32[16,6,8,128]{3,2,1,0:T(8,128)}), f32[16,6,8,128]{3,2,1,0:T(8,128)S(1)}, u32[]{:S(2)}, u32[]{:S(2)}) async-start(f32[16,6,8,128]{3,2,1,0:T(8,128)} %broadcast_in_dim.32), calls=%async_computation.4 | async-start | bytes 786432 | tf_op jit(solution)/shard_map/all_to_all | solution.py:250
  69.3 8.2 %all-to-all-done.4 = f32[16,6,8,128]{3,2,1,0:T(8,128)S(1)} async-done(((f32[16,6,8,128]{3,2,1,0:T(8,128)}), f32[16,6,8,128]{3,2,1,0:T(8,128)S(1)}, u32[]{:S(2)}, u32[]{:S(2)}) %all-to-all-start.4) | async-done | bytes 393248 | tf_op jit(solution)/shard_map/all_to_all | solution.py:250
  77.5 1.1 %broadcast_in_dim.31 = f32[8,2,32,512]{3,2,1,0:T(8,128)} broadcast(f32[2,32,512]{2,1,0:T(8,128)S(1)} %bitcast.36), dimensions={1,2,3} | broadcast | bytes 1179648 | tf_op jit(solution)/shard_map/broadcast_in_dim | solution.py:213
  78.6 9.3 %all-to-all-start.3 = ((f32[8,2,32,512]{3,2,1,0:T(8,128)}), f32[8,2,32,512]{3,2,1,0:T(8,128)S(1)}, u32[]{:S(2)}, u32[]{:S(2)}) async-start(f32[8,2,32,512]{3,2,1,0:T(8,128)} %broadcast_in_dim.31), calls=%async_computation.3 | async-start | bytes 2097152 | tf_op jit(solution)/shard_map/all_to_all | solution.py:253
  87.8 2.4 %all-gather = f32[32,6,8,128]{3,2,1,0:T(8,128)S(1)} all-gather(f32[16,6,8,128]{3,2,1,0:T(8,128)S(1)} %all-to-all-done.4), channel_id=2, replica_groups=mesh['z'=16,'y'=4,'core'=2,'x'=4] {'core'}, dimensions={0}, use_global_device_ids=true | all-gather | bytes 1179648 | tf_op jit(solution)/shard_map/all_gather | solution.py:251
  90.2 0.0 copy-start
  90.2 0.0 copy-start.2
  90.2 12.6 %shard_map.59.solver = f32[3,256,256]{2,1,0:T(8,128)S(1)} custom-call(f32[2,4,4,6,8,128]{5,4,3,2,1,0:T(8,128)S(1)} %bitcast.32), custom_call_target="tpu_custom_call" | custom-call | flops 17179869184 | bytes 1048576 | tf_op jit(solution)/shard_map/pallas_call | solution.py:201
  102.8 0.1 all-to-all-done.3.targets
  103.0 0.0 copy-start.3
  103.0 0.0 copy-done
  103.0 0.0 copy-done.2
  103.0 0.7 copy-done.3
  103.6 4.2 %shard_map.60 = (f32[256,512]{1,0:T(8,128)}, f32[256,512]{1,0:T(8,128)}) custom-call(s32[1]{0:T(128)} %bitcast.row_ref, s32[2]{0:T(128)S(1)} %copy-done.1, s32[2,128]{1,0:T(2,128)S(1)} %copy-done.3, f32[8,2,32,512]{3,2,1,0:T(8,128)S(1)} %all-to-all-done.3.targets, f32[3,256,256]{2,1,0:T(8,128)S(1)} %shard_map.59.solver, f32[256,512]{1,0:T(8,128)S(1)} %bitcast.34, ...), custom_call_target="tpu_custom_call" | custom-call | flops 1073741824 | bytes 1048576 | tf_op jit(solution)/shard_map/pallas_call | solution.py:201
  (18 shorter events, 0.2 us)
Async XLA Ops:
  0.6 19.8 %all-to-all-start = ((f32[8,32,512]{2,1,0:T(8,128)}), f32[8,32,512]{2,1,0:T(8,128)S(1)}, u32[]{:S(2)}, u32[]{:S(2)}) async-start(f32[8,32,512]{2,1,0:T(8,128)} %bitcast.33), calls=%async_computation | async-start | bytes 1048576 | tf_op jit(solution)/shard_map/all_to_all | solution.py:231
  10.9 0.7 copy-start.1
  21.3 22.8 %all-to-all-start.1 = ((f32[16,5,4,128]{3,2,1,0:T(4,128)}), f32[16,5,4,128]{3,2,1,0:T(4,128)S(1)}, u32[]{:S(2)}, u32[]{:S(2)}) async-start(f32[16,5,4,128]{3,2,1,0:T(4,128)} %pad_maximum_fusion), calls=%async_computation.1 | async-start | bytes 327680 | tf_op jit(solution)/shard_map/all_to_all | solution.py:239
  64.5 13.0 %all-to-all-start.4 = ((f32[16,6,8,128]{3,2,1,0:T(8,128)}), f32[16,6,8,128]{3,2,1,0:T(8,128)S(1)}, u32[]{:S(2)}, u32[]{:S(2)}) async-start(f32[16,6,8,128]{3,2,1,0:T(8,128)} %broadcast_in_dim.32), calls=%async_computation.4 | async-start | bytes 786432 | tf_op jit(solution)/shard_map/all_to_all | solution.py:250
  78.6 24.4 %all-to-all-start.3 = ((f32[8,2,32,512]{3,2,1,0:T(8,128)}), f32[8,2,32,512]{3,2,1,0:T(8,128)S(1)}, u32[]{:S(2)}, u32[]{:S(2)}) async-start(f32[8,2,32,512]{3,2,1,0:T(8,128)} %broadcast_in_dim.31), calls=%async_computation.3 | async-start | bytes 2097152 | tf_op jit(solution)/shard_map/all_to_all | solution.py:253
  90.2 12.8 %copy-start = (f32[1,256,512]{2,1,0:T(8,128)S(1)}, f32[1,256,512]{2,1,0:T(8,128)}, u32[]{:S(2)}) copy-start(f32[1,256,512]{2,1,0:T(8,128)} %param.4) | copy-start | bytes 1572868
  90.2 12.8 %copy-start.2 = (f32[1,256,512]{2,1,0:T(8,128)S(1)}, f32[1,256,512]{2,1,0:T(8,128)}, u32[]{:S(2)}) copy-start(f32[1,256,512]{2,1,0:T(8,128)} %param.5) | copy-start | bytes 1572868
  103.0 0.7 copy-start.3

commit v10 on v8

--- a/solution.py
+++ b/solution.py
@@ -167,9 +167,9 @@
     half = width // 2
     row = row_ref[0]
     w00, l10, w11 = split(solver[0]), split(solver[1]), split(solver[2])
-    one = dot6(split(own[:, :half] * flag(pattern, 0, row)), w00)
-    inner = own[:, half:] * flag(pattern, 1, row) - dot6(split(one), l10)
-    two = dot6(split(inner), w11)
+    one = dot3(split(own[:, :half] * flag(pattern, 0, row)), w00)
+    inner = own[:, half:] * flag(pattern, 1, row) - dot3(split(one), l10)
+    two = dot3(split(inner), w11)
     shape = (size, half)
     upper = lax.broadcasted_iota(jnp.int32, shape, 0) < lax.broadcasted_iota(jnp.int32, shape, 1)
     one = jnp.where(upper & (row == 0), 0.0, one)

time: 108 us -> 108 us (level)
  no operation moved by 1% of the time
where the time goes in v10:
time: 108 us
  starting transfers between devices  34.9 us (32%)
  waiting for transfers between devices  23.5 us (22%)
  blocking collectives  21.9 us (20%)
  Pallas kernels  16.6 us (15%)
  between operations  5.93 us (5%)
  local copies, waits for them, and re-layouts  4.02 us (4%)
    all_to_all x1, blocking collectives, local(): part = lax.all_to_all(copies(part, nz), 'z', 0, 0)  19.5 us
    pallas_call x2, Pallas kernels, call(): pl.pallas_call(kernel, in_specs=specs, out_specs=[pl.BlockSpec(memory_spa...  16.6 us
    all_to_all x1, waiting for transfers between devices, local(): got = lax.all_to_all(part, 'z', 0, 0)  10.9 us
    all_to_all x1, starting transfers between devices, local(): got = lax.all_to_all(part, 'z', 0, 0)  10.6 us
    all_to_all x1, starting transfers between devices, local(): pieces = lax.all_to_all(own.reshape(npl, coarse, width), plane, 0, 0)  10.3 us
    all_to_all x1, starting transfers between devices, local(): targets = lax.all_to_all(copies(held, npl), plane, 0, 0)  9.27 us
    all_to_all x1, waiting for transfers between devices, local(): blocks = lax.all_to_all(copies(share, LINES * nx), ('y', 'x'), 0, 0)  8.2 us
    all_to_all x1, starting transfers between devices, local(): blocks = lax.all_to_all(copies(share, LINES * nx), ('y', 'x'), 0, 0)  4.73 us
  transfers between devices with their start and end apart: 4, of which 4 were waited for; matrix products, arithmetic and copies ran while one was open for 1% of the time, Pallas kernels for 12%

profile of v10, /device:TPU:1, one launch (start us, length us, event | category | flops | bytes accessed | tf_op | source)
XLA Modules:
  0.0 107.6 jit_solution(16805817132188999245)
XLA Ops:
  0.6 10.3 %all-to-all-start = ((f32[8,32,512]{2,1,0:T(8,128)}), f32[8,32,512]{2,1,0:T(8,128)S(1)}, u32[]{:S(2)}, u32[]{:S(2)}) async-start(f32[8,32,512]{2,1,0:T(8,128)} %bitcast.33), calls=%async_computation | async-start | bytes 1048576 | tf_op jit(solution)/shard_map/all_to_all | solution.py:223
  10.9 0.0 copy-start.1
  10.9 0.7 copy-done.1
  11.6 0.6 fusion
  16.1 4.4 %all-to-all-done = f32[8,32,512]{2,1,0:T(8,128)S(1)} async-done(((f32[8,32,512]{2,1,0:T(8,128)}), f32[8,32,512]{2,1,0:T(8,128)S(1)}, u32[]{:S(2)}, u32[]{:S(2)}) %all-to-all-start) | async-done | bytes 524320 | tf_op jit(solution)/shard_map/all_to_all | solution.py:223
  20.6 0.7 pad_maximum_fusion
  21.3 10.6 %all-to-all-start.1 = ((f32[16,5,4,128]{3,2,1,0:T(4,128)}), f32[16,5,4,128]{3,2,1,0:T(4,128)S(1)}, u32[]{:S(2)}, u32[]{:S(2)}) async-start(f32[16,5,4,128]{3,2,1,0:T(4,128)} %pad_maximum_fusion), calls=%async_computation.1 | async-start | bytes 327680 | tf_op jit(solution)/shard_map/all_to_all | solution.py:231
  33.2 10.9 %all-to-all-done.1 = f32[16,5,4,128]{3,2,1,0:T(4,128)S(1)} async-done(((f32[16,5,4,128]{3,2,1,0:T(4,128)}), f32[16,5,4,128]{3,2,1,0:T(4,128)S(1)}, u32[]{:S(2)}, u32[]{:S(2)}) %all-to-all-start.1) | async-done | bytes 163872 | tf_op jit(solution)/shard_map/all_to_all | solution.py:231
  44.1 19.5 %all_to_all.25 = f32[16,5,4,128]{3,2,1,0:T(4,128)S(1)} all-to-all(f32[16,5,4,128]{3,2,1,0:T(4,128)S(1)} %broadcast_in_dim.29), channel_id=1, replica_groups=mesh['z'=16,'y'=4,'core'=2,'x'=4] {'z'}, dimensions={0} | all-to-all | bytes 327680 | tf_op jit(solution)/shard_map/all_to_all | solution.py:237
  63.7 0.8 broadcast_in_dim.32
  64.5 4.7 %all-to-all-start.4 = ((f32[16,6,8,128]{3,2,1,0:T(8,128)}), f32[16,6,8,128]{3,2,1,0:T(8,128)S(1)}, u32[]{:S(2)}, u32[]{:S(2)}) async-start(f32[16,6,8,128]{3,2,1,0:T(8,128)} %broadcast_in_dim.32), calls=%async_computation.4 | async-start | bytes 786432 | tf_op jit(solution)/shard_map/all_to_all | solution.py:242
  69.3 8.2 %all-to-all-done.4 = f32[16,6,8,128]{3,2,1,0:T(8,128)S(1)} async-done(((f32[16,6,8,128]{3,2,1,0:T(8,128)}), f32[16,6,8,128]{3,2,1,0:T(8,128)S(1)}, u32[]{:S(2)}, u32[]{:S(2)}) %all-to-all-start.4) | async-done | bytes 393248 | tf_op jit(solution)/shard_map/all_to_all | solution.py:242
  77.5 1.1 %broadcast_in_dim.31 = f32[8,2,32,512]{3,2,1,0:T(8,128)} broadcast(f32[2,32,512]{2,1,0:T(8,128)S(1)} %bitcast.36), dimensions={1,2,3} | broadcast | bytes 1179648 | tf_op jit(solution)/shard_map/broadcast_in_dim | solution.py:205
  78.6 9.3 %all-to-all-start.3 = ((f32[8,2,32,512]{3,2,1,0:T(8,128)}), f32[8,2,32,512]{3,2,1,0:T(8,128)S(1)}, u32[]{:S(2)}, u32[]{:S(2)}) async-start(f32[8,2,32,512]{3,2,1,0:T(8,128)} %broadcast_in_dim.31), calls=%async_computation.3 | async-start | bytes 2097152 | tf_op jit(solution)/shard_map/all_to_all | solution.py:245
  87.8 2.4 %all-gather = f32[32,6,8,128]{3,2,1,0:T(8,128)S(1)} all-gather(f32[16,6,8,128]{3,2,1,0:T(8,128)S(1)} %all-to-all-done.4), channel_id=2, replica_groups=mesh['z'=16,'y'=4,'core'=2,'x'=4] {'core'}, dimensions={0}, use_global_device_ids=true | all-gather | bytes 1179648 | tf_op jit(solution)/shard_map/all_gather | solution.py:243
  90.2 0.0 copy-start
  90.2 0.0 copy-start.2
  90.2 12.6 %shard_map.59.solver = f32[3,256,256]{2,1,0:T(8,128)S(1)} custom-call(f32[2,4,4,6,8,128]{5,4,3,2,1,0:T(8,128)S(1)} %bitcast.32), custom_call_target="tpu_custom_call" | custom-call | flops 17179869184 | bytes 1048576 | tf_op jit(solution)/shard_map/pallas_call | solution.py:194
  102.8 0.1 all-to-all-done.3.targets
  103.0 0.0 copy-start.3
  103.0 0.0 copy-done
  103.0 0.0 copy-done.2
  103.0 0.7 copy-done.3
  103.6 3.9 %shard_map.60 = (f32[256,512]{1,0:T(8,128)}, f32[256,512]{1,0:T(8,128)}) custom-call(s32[1]{0:T(128)} %bitcast.row_ref, s32[2,128]{1,0:T(2,128)S(1)} %copy-done.3, s32[2]{0:T(128)S(1)} %copy-done.1, f32[8,2,32,512]{3,2,1,0:T(8,128)S(1)} %all-to-all-done.3.targets, f32[3,256,256]{2,1,0:T(8,128)S(1)} %shard_map.59.solver, f32[256,512]{1,0:T(8,128)S(1)} %bitcast.34, ...), custom_call_target="tpu_custom_call" | custom-call | flops 1073741824 | bytes 1048576 | tf_op jit(solution)/shard_map/pallas_call | solution.py:194
  (18 shorter events, 0.2 us)
Async XLA Ops:
  0.6 19.8 %all-to-all-start = ((f32[8,32,512]{2,1,0:T(8,128)}), f32[8,32,512]{2,1,0:T(8,128)S(1)}, u32[]{:S(2)}, u32[]{:S(2)}) async-start(f32[8,32,512]{2,1,0:T(8,128)} %bitcast.33), calls=%async_computation | async-start | bytes 1048576 | tf_op jit(solution)/shard_map/all_to_all | solution.py:223
  10.9 0.7 copy-start.1
  21.3 22.8 %all-to-all-start.1 = ((f32[16,5,4,128]{3,2,1,0:T(4,128)}), f32[16,5,4,128]{3,2,1,0:T(4,128)S(1)}, u32[]{:S(2)}, u32[]{:S(2)}) async-start(f32[16,5,4,128]{3,2,1,0:T(4,128)} %pad_maximum_fusion), calls=%async_computation.1 | async-start | bytes 327680 | tf_op jit(solution)/shard_map/all_to_all | solution.py:231
  64.5 13.0 %all-to-all-start.4 = ((f32[16,6,8,128]{3,2,1,0:T(8,128)}), f32[16,6,8,128]{3,2,1,0:T(8,128)S(1)}, u32[]{:S(2)}, u32[]{:S(2)}) async-start(f32[16,6,8,128]{3,2,1,0:T(8,128)} %broadcast_in_dim.32), calls=%async_computation.4 | async-start | bytes 786432 | tf_op jit(solution)/shard_map/all_to_all | solution.py:242
  78.6 24.4 %all-to-all-start.3 = ((f32[8,2,32,512]{3,2,1,0:T(8,128)}), f32[8,2,32,512]{3,2,1,0:T(8,128)S(1)}, u32[]{:S(2)}, u32[]{:S(2)}) async-start(f32[8,2,32,512]{3,2,1,0:T(8,128)} %broadcast_in_dim.31), calls=%async_computation.3 | async-start | bytes 2097152 | tf_op jit(solution)/shard_map/all_to_all | solution.py:245
  90.2 12.8 %copy-start = (f32[1,256,512]{2,1,0:T(8,128)S(1)}, f32[1,256,512]{2,1,0:T(8,128)}, u32[]{:S(2)}) copy-start(f32[1,256,512]{2,1,0:T(8,128)} %param.4) | copy-start | bytes 1572868
  90.2 12.8 %copy-start.2 = (f32[1,256,512]{2,1,0:T(8,128)S(1)}, f32[1,256,512]{2,1,0:T(8,128)}, u32[]{:S(2)}) copy-start(f32[1,256,512]{2,1,0:T(8,128)} %param.5) | copy-start | bytes 1572868
  103.0 0.7 copy-start.3
